TPU v7x, 32 devices: a whole 2x2x4 slice. The times are simulated.
32 devices in a mesh: grp: 2 (over x), lon: 16 (over z, y, core).
Axes of the slice: x: 2, y: 2, z: 4, core: 2. Of those that a mesh axis runs over, the one named last changes fastest.
Arguments:
- fields: bfloat16 [64, 1536, 256], P('grp', 'lon'), parts along dimension 0, may hold values from -6 to 6
- zonal_coef: bfloat16 [32, 1536], replicated, may hold values from -0.15625 to 0.15625
- vert_taps: bfloat16 [15], replicated, may hold values from 0.019897461 to 0.14941406
Outputs:
- filtered: bfloat16 [64, 1536, 256], P('grp', 'lon'), parts along dimension 0
There are 2 independent parts, one for each index of `grp`. A program takes and returns all parts, laid end to end along the dimension named above; an argument that names none is the same for every part. Nothing has to cross between parts.
All inputs are finite; a program needn't handle non-finite values.
Results may differ from a plain program's by a relative error of at most 0.0049.
Values may be sent and summed in bfloat16 or wider, within the bound.
No kernel may reach another device: no remote copies, remote signals or barrier semaphores. Data moves between devices by JAX's collectives and lax.ppermute only.
A program may use at most 128 MiB of HBM per device.

v0:
```python
import functools

import jax
import jax.numpy as jnp
from jax import lax
from jax.experimental import pallas as pl
from jax.experimental.pallas import tpu as pltpu
from jax.sharding import PartitionSpec as P

LEV = 64
TAPS = 15
LANES = 128
WIDE = 256
STEPS = 2
VMEM = pl.BlockSpec(memory_space=pltpu.VMEM)
SMEM = pl.BlockSpec(memory_space=pltpu.SMEM)
PARAMS = pltpu.CompilerParams(vmem_limit_bytes=32 * 1024 * 1024)


def circulant_kernel(coef_ref, circ_ref):
    lats, n = coef_ref.shape
    for a in range(lats):
        row = coef_ref[a : a + 1].astype(jnp.float32)
        rolled = pltpu.roll(
            jnp.broadcast_to(row, (LANES, n)), 0, 1, stride=1, stride_axis=0
        )
        first = rolled.T.astype(jnp.bfloat16)
        circ_ref[a, :, :LANES] = first
        circ_ref[a, LANES:, LANES:] = first[: n - LANES]
        circ_ref[a, :LANES, LANES:] = first[n - LANES :]


def circulant(coef):
    lats, n = coef.shape
    return pl.pallas_call(
        circulant_kernel,
        in_specs=[VMEM],
        out_specs=VMEM,
        out_shape=jax.ShapeDtypeStruct((lats, n, WIDE), jnp.bfloat16),
        compiler_params=PARAMS,
        cost_estimate=pl.CostEstimate(
            flops=16 * lats * n * LANES, bytes_accessed=2 * lats * n * WIDE, transcendentals=0
        ),
    )(coef)


def zonal_kernel(circ_ref, x_ref, o_ref):
    parts, lats, count, columns = x_ref.shape
    n = parts * count
    for a in range(lats):
        x = x_ref[:, a].reshape(n, columns)
        first = circ_ref[a]
        circ = jnp.concatenate(
            [first] + [jnp.concatenate([first[n - j :], first[: n - j]]) for j in range(WIDE, n, WIDE)],
            axis=1,
        )
        total = jnp.dot(circ, x, preferred_element_type=jnp.float32)
        o_ref[:, a] = total.astype(jnp.bfloat16).reshape(parts, count, columns)


def zonal(circ, x):
    parts, lats, count, columns = x.shape
    n = parts * count
    return pl.pallas_call(
        zonal_kernel,
        in_specs=[VMEM, VMEM],
        out_specs=VMEM,
        out_shape=jax.ShapeDtypeStruct(x.shape, jnp.bfloat16),
        compiler_params=PARAMS,
        cost_estimate=pl.CostEstimate(
            flops=2 * lats * n * n * columns, bytes_accessed=2 * lats * n * n, transcendentals=0
        ),
    )(circ, x)


def band_kernel(taps_ref, band_ref):
    half = (TAPS - 1) // 2
    upper = lax.broadcasted_iota(jnp.int32, band_ref.shape, 0)
    lower = lax.broadcasted_iota(jnp.int32, band_ref.shape, 1)
    offset = jnp.where(upper // LEV == lower // LEV, upper - lower, TAPS)
    band = jnp.zeros(band_ref.shape, jnp.float32)
    for tap in range(TAPS):
        band = jnp.where(offset == tap - half, taps_ref[tap], band)
    band_ref[...] = band.astype(jnp.bfloat16)


def band_matrix(taps, columns):
    return pl.pallas_call(
        band_kernel,
        in_specs=[SMEM],
        out_specs=VMEM,
        out_shape=jax.ShapeDtypeStruct((columns, columns), jnp.bfloat16),
        compiler_params=PARAMS,
    )(taps)


def vertical_kernel(band_ref, x_ref, o_ref):
    rows, count, columns = o_ref.shape
    x = x_ref[pl.ds(pl.program_id(0) * rows, rows)].reshape(rows * count, columns)
    mixed = jnp.dot(x, band_ref[...], preferred_element_type=jnp.float32)
    o_ref[...] = mixed.astype(jnp.bfloat16).reshape(o_ref.shape)


def vertical(band, x):
    lat_rows, count, columns = x.shape
    rows = lat_rows // STEPS
    return pl.pallas_call(
        vertical_kernel,
        grid=(STEPS,),
        in_specs=[VMEM, VMEM],
        out_specs=pl.BlockSpec((rows, count, columns), lambda i: (i, 0, 0)),
        out_shape=jax.ShapeDtypeStruct(x.shape, jnp.bfloat16),
        compiler_params=PARAMS,
        cost_estimate=pl.CostEstimate(
            flops=2 * x.size * columns, bytes_accessed=4 * x.size, transcendentals=0
        ),
    )(band, x)


def shards(fields, zonal_coef, vert_taps, *, parts):
    lat_rows, count, columns = fields.shape
    lats = lat_rows // parts
    me = lax.axis_index("lon")
    swapped = lambda x: lax.all_to_all(x, "lon", 0, 0, tiled=True)
    circ = circulant(lax.dynamic_slice_in_dim(zonal_coef, me * lats, lats, 0))
    mine = swapped(fields).reshape(parts, lats, count, columns)
    done = zonal(circ, mine)
    done, taps = lax.optimization_barrier((done, vert_taps.astype(jnp.float32)))
    band = band_matrix(taps, columns)
    return vertical(band, swapped(done.reshape(fields.shape)))


def solution(mesh):
    placed = (P("grp", "lon", None), P(), P())
    return jax.shard_map(
        functools.partial(shards, parts=mesh.shape["lon"]),
        mesh=mesh,
        in_specs=placed,
        out_specs=P("grp", "lon", None),
        check_vma=False,
    )
```

profile of v0, /device:TPU:15, one launch (start us, length us, event | category | flops | bytes accessed | tf_op | source)
XLA Modules:
  0.0 89.4 jit_solution(1633959947612747942)
XLA Ops:
  0.0 0.0 copy-start
  0.0 0.0 copy-start.1
  0.0 6.7 %all-to-all-start = ((bf16[32,96,256]{2,1,0:T(8,128)(2,1)}), bf16[32,96,256]{2,1,0:T(8,128)(2,1)S(1)}, u32[]{:S(2)}, u32[]{:S(2)}) async-start(bf16[32,96,256]{2,1,0:T(8,128)(2,1)} %param.3), calls=%async_computation | async-start | bytes 3145728 | tf_op jit(solution)/shard_map/all_to_all | solution.py:124
  6.7 0.0 copy-done.1
  6.7 0.0 copy-done
  6.7 0.5 shard_map.37.circ_ref
  7.3 35.6 %all-to-all-done = bf16[32,96,256]{2,1,0:T(8,128)(2,1)S(1)} async-done(((bf16[32,96,256]{2,1,0:T(8,128)(2,1)}), bf16[32,96,256]{2,1,0:T(8,128)(2,1)S(1)}, u32[]{:S(2)}, u32[]{:S(2)}) %all-to-all-start) | async-done | bytes 1572896 | tf_op jit(solution)/shard_map/all_to_all | solution.py:124
  42.9 3.8 %shard_map.38 = bf16[16,2,96,256]{3,2,1,0:T(8,128)(2,1)} custom-call(bf16[2,1536,256]{2,1,0:T(8,128)(2,1)S(1)} %shard_map.37.circ_ref, bf16[16,2,96,256]{3,2,1,0:T(8,128)(2,1)S(1)} %bitcast.2), custom_call_target="tpu_custom_call" | custom-call | flops 2415919104 | bytes 9437184 | tf_op jit(solution)/shard_map/pallas_call | solution.py:64
  46.7 4.9 %all-to-all-start.1 = ((bf16[32,96,256]{2,1,0:T(8,128)(2,1)}), bf16[32,96,256]{2,1,0:T(8,128)(2,1)S(1)}, u32[]{:S(2)}, u32[]{:S(2)}) async-start(bf16[32,96,256]{2,1,0:T(8,128)(2,1)} %bitcast.1), calls=%async_computation.1 | async-start | bytes 3145728 | tf_op jit(solution)/shard_map/all_to_all | solution.py:124
  51.6 0.8 shard_map.39.band_ref
  52.4 35.4 %all-to-all-done.1.x_ref = bf16[32,96,256]{2,1,0:T(8,128)(2,1)S(1)} async-done(((bf16[32,96,256]{2,1,0:T(8,128)(2,1)}), bf16[32,96,256]{2,1,0:T(8,128)(2,1)S(1)}, u32[]{:S(2)}, u32[]{:S(2)}) %all-to-all-start.1) | async-done | bytes 1572896 | tf_op jit(solution)/shard_map/all_to_all | solution.py:124
  87.8 1.6 %shard_map.40 = bf16[32,96,256]{2,1,0:T(8,128)(2,1)} custom-call(bf16[256,256]{1,0:T(8,128)(2,1)S(1)} %shard_map.39.band_ref, bf16[32,96,256]{2,1,0:T(8,128)(2,1)S(1)} %all-to-all-done.1.x_ref), custom_call_target="tpu_custom_call" | custom-call | flops 402653184 | bytes 3145728 | tf_op jit(solution)/shard_map/pallas_call | solution.py:107
  (2 shorter events, 0.0 us)
Async XLA Ops:
  0.0 6.7 %copy-start = (bf16[32,1536]{1,0:T(8,128)(2,1)S(1)}, bf16[32,1536]{1,0:T(8,128)(2,1)}, u32[]{:S(2)}) copy-start(bf16[32,1536]{1,0:T(8,128)(2,1)} %param.4) | copy-start | bytes 294916
  0.0 6.7 %copy-start.1 = (bf16[15]{0:T(256)(128)(2,1)S(1)}, bf16[15]{0:T(256)(128)(2,1)}, u32[]{:S(2)}) copy-start(bf16[15]{0:T(256)(128)(2,1)} %param.5) | copy-start | bytes 94
  0.0 42.9 %all-to-all-start = ((bf16[32,96,256]{2,1,0:T(8,128)(2,1)}), bf16[32,96,256]{2,1,0:T(8,128)(2,1)S(1)}, u32[]{:S(2)}, u32[]{:S(2)}) async-start(bf16[32,96,256]{2,1,0:T(8,128)(2,1)} %param.3), calls=%async_computation | async-start | bytes 3145728 | tf_op jit(solution)/shard_map/all_to_all | solution.py:124
  46.7 41.1 %all-to-all-start.1 = ((bf16[32,96,256]{2,1,0:T(8,128)(2,1)}), bf16[32,96,256]{2,1,0:T(8,128)(2,1)S(1)}, u32[]{:S(2)}, u32[]{:S(2)}) async-start(bf16[32,96,256]{2,1,0:T(8,128)(2,1)} %bitcast.1), calls=%async_computation.1 | async-start | bytes 3145728 | tf_op jit(solution)/shard_map/all_to_all | solution.py:124
where the time goes:
time: 89.7 us; the launch traced here: 89.4 us
  waiting for transfers between devices  71 us (79%)
  starting transfers between devices  11.6 us (13%)
  Pallas kernels  6.73 us (8%)
    all_to_all x2, waiting for transfers between devices, shards(): swapped = lambda x: lax.all_to_all(x, 'lon', 0, 0, tiled=True)  71 us
    all_to_all x2, starting transfers between devices, shards(): swapped = lambda x: lax.all_to_all(x, 'lon', 0, 0, tiled=True)  11.6 us
    pallas_call x1, Pallas kernels, zonal(): pl.pallas_call(zonal_kernel, in_specs=[VMEM, VMEM], out_specs=VMEM, out_s...  3.83 us
  transfers between devices with their start and end apart: 2, of which 2 were waited for; matrix products, arithmetic and copies ran while one was open for 0% of the time, Pallas kernels for 1%

commit v1 on v0

--- a/solution.py
+++ b/solution.py
@@ -12,6 +12,8 @@
 LANES = 128
 WIDE = 256
 STEPS = 2
+NEAR = 4
+HBM = pl.BlockSpec(memory_space=pltpu.HBM)
 VMEM = pl.BlockSpec(memory_space=pltpu.VMEM)
 SMEM = pl.BlockSpec(memory_space=pltpu.SMEM)
 PARAMS = pltpu.CompilerParams(vmem_limit_bytes=32 * 1024 * 1024)
@@ -117,9 +119,222 @@
     )(band, x)
 
 
+def copied(copies):
+    for copy in copies:
+        copy.start()
+    for copy in copies:
+        copy.wait()
+
+
+def first_half_kernel(x_ref, o_ref, sem):
+    copied([pltpu.make_async_copy(x_ref.at[pl.ds(0, o_ref.shape[0])], o_ref, sem.at[0])])
+
+
+def first_half(x):
+    lat_rows, count, columns = x.shape
+    return pl.pallas_call(
+        first_half_kernel,
+        in_specs=[HBM],
+        out_specs=VMEM,
+        out_shape=jax.ShapeDtypeStruct((lat_rows // 2, count, columns), jnp.bfloat16),
+        scratch_shapes=[pltpu.SemaphoreType.DMA((1,))],
+        compiler_params=PARAMS,
+    )(x)
+
+
+def second_half_kernel(me_ref, x_ref, *refs):
+    outs, sem = refs[:-1], refs[-1]
+    half = len(outs) * NEAR
+    copies = []
+    for r in range(half):
+        x = x_ref.at[half + (me_ref[0] ^ r)]
+        out = outs[r // NEAR].at[r % NEAR]
+        copies.append(pltpu.make_async_copy(x, out, sem.at[r]))
+    copied(copies)
+
+
+def second_half(me, x):
+    lat_rows, count, columns = x.shape
+    arrays = lat_rows // 2 // NEAR
+    return pl.pallas_call(
+        second_half_kernel,
+        in_specs=[SMEM, HBM],
+        out_specs=[VMEM] * arrays,
+        out_shape=[jax.ShapeDtypeStruct((NEAR, count, columns), jnp.bfloat16)] * arrays,
+        scratch_shapes=[pltpu.SemaphoreType.DMA((lat_rows // 2,))],
+        compiler_params=PARAMS,
+    )(me, x)
+
+
+def rotations(first):
+    n, wide = first.shape
+    turned = [jnp.concatenate([first[n - j :], first[: n - j]]) for j in range(wide, n, wide)]
+    return jnp.concatenate([first] + turned, axis=1)
+
+
+def zonal_first_kernel(circ_ref, x_ref, o_ref):
+    parts, count, columns = x_ref.shape
+    x = x_ref[...].reshape(parts * count, columns)
+    total = jnp.dot(rotations(circ_ref[0]), x, preferred_element_type=jnp.float32)
+    o_ref[...] = total.astype(jnp.bfloat16).reshape(o_ref.shape)
+
+
+def zonal_cost(circ, columns):
+    n = circ.shape[1]
+    return pl.CostEstimate(
+        flops=2 * n * n * columns, bytes_accessed=2 * n * n, transcendentals=0
+    )
+
+
+def zonal_first(circ, x):
+    return pl.pallas_call(
+        zonal_first_kernel,
+        in_specs=[VMEM, VMEM],
+        out_specs=VMEM,
+        out_shape=jax.ShapeDtypeStruct(x.shape, jnp.bfloat16),
+        compiler_params=PARAMS,
+        cost_estimate=zonal_cost(circ, x.shape[2]),
+    )(circ, x)
+
+
+def distance_of(core, i, far):
+    return i % far * NEAR + i // far * 2 + core
+
+
+def zonal_second_kernel(me_ref, circ_ref, *refs):
+    ins, outs, (x, z) = refs[:2], refs[2:-2], refs[-2:]
+    parts, count, columns = x.shape
+    for core in range(2):
+        for i in range(parts // 2):
+            r = distance_of(core, i, len(outs))
+            x[me_ref[0] ^ r] = ins[core][i]
+    total = jnp.dot(
+        rotations(circ_ref[1]),
+        x[...].reshape(parts * count, columns),
+        preferred_element_type=jnp.float32,
+    )
+    z[...] = total.astype(jnp.bfloat16).reshape(z.shape)
+    for r in range(parts):
+        outs[r // NEAR][r % NEAR] = z[me_ref[0] ^ r]
+
+
+def zonal_second(me, circ, blocks):
+    half, count, columns = blocks[0].shape
+    arrays = 2 * half // NEAR
+    return pl.pallas_call(
+        zonal_second_kernel,
+        in_specs=[SMEM] + [VMEM] * 3,
+        out_specs=[VMEM] * arrays,
+        out_shape=[jax.ShapeDtypeStruct((NEAR, count, columns), jnp.bfloat16)] * arrays,
+        scratch_shapes=[pltpu.VMEM((2 * half, count, columns), jnp.bfloat16)] * 2,
+        compiler_params=PARAMS,
+        cost_estimate=zonal_cost(circ, columns),
+    )(me, circ, *blocks)
+
+
+def vertical_first_kernel(band_ref, x_ref, _, o_ref):
+    x = x_ref[...].reshape(-1, x_ref.shape[2])
+    mixed = jnp.dot(x, band_ref[...], preferred_element_type=jnp.float32)
+    o_ref[...] = mixed.astype(jnp.bfloat16).reshape(o_ref.shape)
+
+
+def vertical_first(band, x, result):
+    parts, count, columns = x.shape
+    rows = parts // STEPS
+    return pl.pallas_call(
+        vertical_first_kernel,
+        grid=(STEPS,),
+        in_specs=[VMEM, pl.BlockSpec((rows, count, columns), lambda i: (i, 0, 0)), HBM],
+        out_specs=pl.BlockSpec((rows, count, columns), lambda i: (i, 0, 0)),
+        out_shape=jax.ShapeDtypeStruct(result.shape, jnp.bfloat16),
+        input_output_aliases={2: 0},
+        compiler_params=PARAMS,
+    )(band, x, result)
+
+
+def vertical_second_kernel(me_ref, band_ref, *refs):
+    ins, (o_ref, mixed, sem) = refs[:2], refs[2:]
+    parts, count, columns = mixed.shape
+    half = parts // 2
+    copies = []
+    for core in range(2):
+        x = ins[core][...].reshape(half * count, columns)
+        out = jnp.dot(x, band_ref[...], preferred_element_type=jnp.float32)
+        out = out.astype(jnp.bfloat16).reshape(ins[core].shape)
+        mixed[core * half : (core + 1) * half] = out
+        for i in range(half):
+            lat = parts + (me_ref[0] ^ distance_of(core, i, parts // NEAR))
+            block = core * half + i
+            copy = pltpu.make_async_copy(mixed.at[block], o_ref.at[lat], sem.at[block])
+            copy.start()
+            copies.append(copy)
+    for copy in copies:
+        copy.wait()
+
+
+def vertical_second(me, band, blocks):
+    half, count, columns = blocks[0].shape
+    return pl.pallas_call(
+        vertical_second_kernel,
+        in_specs=[SMEM] + [VMEM] * 3,
+        out_specs=HBM,
+        out_shape=jax.ShapeDtypeStruct((4 * half, count, columns), jnp.bfloat16),
+        scratch_shapes=[
+            pltpu.VMEM((2 * half, count, columns), jnp.bfloat16),
+            pltpu.SemaphoreType.DMA((2 * half,)),
+        ],
+        compiler_params=PARAMS,
+    )(me, band, *blocks)
+
+
+def hop(x, distance, parts):
+    return lax.ppermute(x, "lon", [(i, i ^ distance) for i in range(parts)])
+
+
+def far_hops(arrays, parts):
+    return [arrays[0]] + [hop(arrays[i], i * NEAR, parts) for i in range(1, len(arrays))]
+
+
+def near_hops(arrays, parts):
+    far, shape = len(arrays), arrays[0].shape[1:]
+    state = jnp.stack(arrays).reshape((far, 2, 2) + shape)
+    state = jnp.stack([state[:, 0], hop(state[:, 1], 2, parts)])
+    keep, send = (state[:, :, i].reshape((2 * far,) + shape) for i in range(2))
+    return keep, hop(send, 1, parts)
+
+
+def two_ways(fields, zonal_coef, vert_taps, parts):
+    lat_rows, count, columns = fields.shape
+    position = lax.axis_index("lon")
+    me = position.reshape(1)
+    swapped = lambda x: lax.all_to_all(x, "lon", 0, 0, tiled=True)
+    band = band_matrix(vert_taps.astype(jnp.float32), columns)
+    coef = lax.dynamic_index_in_dim(
+        zonal_coef.reshape(2, parts, -1), position, 1, keepdims=False
+    )
+    circ = circulant(coef)
+    arrays = far_hops(second_half(me, fields), parts)
+    x = first_half(fields)
+    x, _ = lax.optimization_barrier((x, [arrays[3]]))
+    mine = swapped(x)
+    arrays = near_hops(arrays, parts)
+    arrays = zonal_second(me, circ, arrays)
+    mine, _ = lax.optimization_barrier((mine, arrays[0]))
+    arrays = far_hops(arrays, parts)
+    done = zonal_first(circ, mine)
+    _, *after = lax.optimization_barrier((done, *arrays))
+    done, _ = lax.optimization_barrier((done, [arrays[3]]))
+    back = swapped(done)
+    result = vertical_second(me, band, near_hops(after, parts))
+    back, result = lax.optimization_barrier((back, result))
+    return vertical_first(band, back, result)
+
+
 def shards(fields, zonal_coef, vert_taps, *, parts):
     lat_rows, count, columns = fields.shape
     lats = lat_rows // parts
+    if lats == 2 and parts & (parts - 1) == 0 and parts >= NEAR:
+        return two_ways(fields, zonal_coef, vert_taps, parts)
     me = lax.axis_index("lon")
     swapped = lambda x: lax.all_to_all(x, "lon", 0, 0, tiled=True)
     circ = circulant(lax.dynamic_slice_in_dim(zonal_coef, me * lats, lats, 0))

time: 89.7 us -> 87.7 us (0.978)
  the two profiles are of different devices: /device:TPU:15 before, /device:TPU:1 now
where the time goes in v1:
time: 87.7 us; the launch traced here: 87 us
  waiting for transfers between devices  43 us (49%)
  starting transfers between devices  30.6 us (35%)
  Pallas kernels  10.7 us (12%)
  local copies, waits for them, and re-layouts  1.59 us (2%)
  other arithmetic  1.09 us (1%)
    ppermute x10, waiting for transfers between devices, hop(): return lax.ppermute(x, 'lon', [(i, i ^ distance) for i in range(parts)])  43 us
    all_to_all x2, starting transfers between devices, two_ways(): swapped = lambda x: lax.all_to_all(x, 'lon', 0, 0, tiled=True)  18.3 us
    ppermute x10, starting transfers between devices, hop(): return lax.ppermute(x, 'lon', [(i, i ^ distance) for i in range(parts)])  12.3 us
    pallas_call x1, Pallas kernels, zonal_second(): pl.pallas_call(zonal_second_kernel, in_specs=[SMEM] + [VMEM] * 3, out_spe...  2.33 us
    pallas_call x1, Pallas kernels, zonal_first(): pl.pallas_call(zonal_first_kernel, in_specs=[VMEM, VMEM], out_specs=VMEM,...  2.29 us
  transfers between devices with their start and end apart: 12, of which 8 were waited for; matrix products, arithmetic and copies ran while one was open for 1% of the time, Pallas kernels for 9%

profile of v1, /device:TPU:1, one launch (start us, length us, event | category | flops | bytes accessed | tf_op | source)
XLA Modules:
  0.0 87.0 jit_solution(9812587072139290127)
XLA Ops:
  0.0 1.4 %copy-done.1 = bf16[32,96,256]{2,1,0:T(8,128)(2,1)S(1)} copy-done((bf16[32,96,256]{2,1,0:T(8,128)(2,1)S(1)}, bf16[32,96,256]{2,1,0:T(8,128)(2,1)}, u32[]{:S(2)}) %copy-start.1) | copy-done | bytes 1572888
  1.4 1.2 %shard_map.40 = (bf16[4,96,256]{2,1,0:T(8,128)(2,1)S(1)}, bf16[4,96,256]{2,1,0:T(8,128)(2,1)S(1)}, bf16[4,96,256]{2,1,0:T(8,128)(2,1)S(1)}, bf16[4,96,256]{2,1,0:T(8,128)(2,1)S(1)}) custom-call(s32[1]{0:T(128)} %bitcast.2.me_ref, bf16[32,96,256]{2,1,0:T(8,128)(2,1)S(1)} %copy-done.1), custom_call_target="tpu_custom_call" | custom-call | tf_op jit(solution)/shard_map/pallas_call | solution.py:159
  2.6 4.2 %collective-permute-start = (bf16[4,96,256]{2,1,0:T(8,128)(2,1)S(1)}, bf16[4,96,256]{2,1,0:T(8,128)(2,1)S(1)}, u32[]{:S(2)}, u32[]{:S(2)}) collective-permute-start(bf16[4,96,256]{2,1,0:T(8,128)(2,1)S(1)} %get-tuple-element.22), channel_id=1, source_target_pairs={{0,12},{1,13},{2,14},{3,15},{4,8},{5,9},{6,10},{7,11},{8,4},{9,5},... | collective-permute-start | bytes 589832 | tf_op jit(solution)/shard_map/ppermute | solution.py:291
  6.8 0.4 collective-permute-start.2
  7.2 0.9 %shard_map.39 = bf16[16,96,256]{2,1,0:T(8,128)(2,1)} custom-call(bf16[32,96,256]{2,1,0:T(8,128)(2,1)S(1)} %copy-done.1), custom_call_target="tpu_custom_call" | custom-call | tf_op jit(solution)/shard_map/pallas_call | solution.py:135
  8.2 3.4 %collective-permute-done = bf16[4,96,256]{2,1,0:T(8,128)(2,1)S(1)} collective-permute-done((bf16[4,96,256]{2,1,0:T(8,128)(2,1)S(1)}, bf16[4,96,256]{2,1,0:T(8,128)(2,1)S(1)}, u32[]{:S(2)}, u32[]{:S(2)}) %collective-permute-start) | collective-permute-done | bytes 196640 | tf_op jit(solution)/shard_map/ppermute | solution.py:291
  11.5 9.8 %all-to-all-start = ((bf16[16,96,256]{2,1,0:T(8,128)(2,1)}), bf16[16,96,256]{2,1,0:T(8,128)(2,1)S(1)}, u32[]{:S(2)}, u32[]{:S(2)}) async-start(bf16[16,96,256]{2,1,0:T(8,128)(2,1)} %shard_map.39), calls=%async_computation | async-start | bytes 1572864 | tf_op jit(solution)/shard_map/all_to_all | solution.py:310
  21.3 1.8 %collective-permute-done.2 = bf16[4,96,256]{2,1,0:T(8,128)(2,1)S(1)} collective-permute-done((bf16[4,96,256]{2,1,0:T(8,128)(2,1)S(1)}, bf16[4,96,256]{2,1,0:T(8,128)(2,1)S(1)}, u32[]{:S(2)}, u32[]{:S(2)}) %collective-permute-start.2) | collective-permute-done | bytes 196640 | tf_op jit(solution)/shard_map/ppermute | solution.py:291
  23.1 0.1 pad_maximum_fusion
  23.2 0.1 slice_bitcast_fusion.2
  23.3 1.3 %collective-permute-start.3 = (bf16[4,2,96,256]{3,2,0,1:T(8,128)(2,1)S(1)}, bf16[4,2,96,256]{3,2,0,1:T(8,128)(2,1)S(1)}, u32[]{:S(2)}, u32[]{:S(2)}) collective-permute-start(bf16[4,2,96,256]{3,2,0,1:T(8,128)(2,1)S(1)} %get-tuple-element.45), channel_id=1, source_target_pairs={{0,2},{1,3},{2,0},{3,1},{4,6},{5,7},{6,4},{7,5},{8,10},{9,11},{10,... | collective-permute-start | bytes 1179656 | tf_op jit(solution)/shard_map/ppermute | solution.py:291
  24.6 15.9 %collective-permute-done.3 = bf16[4,2,96,256]{3,2,0,1:T(8,128)(2,1)S(1)} collective-permute-done((bf16[4,2,96,256]{3,2,0,1:T(8,128)(2,1)S(1)}, bf16[4,2,96,256]{3,2,0,1:T(8,128)(2,1)S(1)}, u32[]{:S(2)}, u32[]{:S(2)}) %collective-permute-start.3) | collective-permute-done | bytes 393248 | tf_op jit(solution)/shard_map/ppermute | solution.py:291
  40.5 0.8 pad_maximum_fusion.3
  41.4 0.9 %collective-permute-start.4 = (bf16[8,96,256]{2,1,0:T(8,128)(2,1)}, bf16[8,96,256]{2,1,0:T(8,128)(2,1)S(1)}, u32[]{:S(2)}, u32[]{:S(2)}) collective-permute-start(bf16[8,96,256]{2,1,0:T(8,128)(2,1)} %bitcast.16), channel_id=1, source_target_pairs={{0,1},{1,0},{2,3},{3,2},{4,5},{5,4},{6,7},{7,6},{8,9},{9,8},{10,11... | collective-permute-start | bytes 1179656 | tf_op jit(solution)/shard_map/ppermute | solution.py:291
  42.3 0.5 shard_map.38.circ_ref
  42.8 1.0 %collective-permute-done.4.refs_1_ = bf16[8,96,256]{2,1,0:T(8,128)(2,1)S(1)} collective-permute-done((bf16[8,96,256]{2,1,0:T(8,128)(2,1)}, bf16[8,96,256]{2,1,0:T(8,128)(2,1)S(1)}, u32[]{:S(2)}, u32[]{:S(2)}) %collective-permute-start.4) | collective-permute-done | bytes 393248 | tf_op jit(solution)/shard_map/ppermute | solution.py:291
  43.8 2.3 %shard_map.41 = (bf16[4,96,256]{2,1,0:T(8,128)(2,1)S(1)}, bf16[4,96,256]{2,1,0:T(8,128)(2,1)}, bf16[4,96,256]{2,1,0:T(8,128)(2,1)}, bf16[4,96,256]{2,1,0:T(8,128)(2,1)}) custom-call(s32[1]{0:T(128)} %bitcast.2.me_ref, bf16[2,1536,256]{2,1,0:T(8,128)(2,1)S(1)} %shard_map.38.circ_ref, bf16[8,96,256]{2,1,0:T(8,128)(2,1)S(1)} %bitcast.49, ...), custom_call_target="tpu_custom_call" | custom-call | flops 1207959552 | bytes 4718592 | tf_op jit(solution)/shard_map/pallas_call | solution.py:224
  46.1 3.0 %collective-permute-start.5 = (bf16[4,96,256]{2,1,0:T(8,128)(2,1)}, bf16[4,96,256]{2,1,0:T(8,128)(2,1)S(1)}, u32[]{:S(2)}, u32[]{:S(2)}) collective-permute-start(bf16[4,96,256]{2,1,0:T(8,128)(2,1)} %get-tuple-element.29), channel_id=1, source_target_pairs={{0,12},{1,13},{2,14},{3,15},{4,8},{5,9},{6,10},{7,11},{8,4},{9,5},... | collective-permute-start | bytes 589832 | tf_op jit(solution)/shard_map/ppermute | solution.py:291
  49.1 0.6 collective-permute-start.7
  49.7 2.3 %shard_map.42 = bf16[16,96,256]{2,1,0:T(8,128)(2,1)} custom-call(bf16[2,1536,256]{2,1,0:T(8,128)(2,1)S(1)} %shard_map.38.circ_ref, bf16[16,96,256]{2,1,0:T(8,128)(2,1)S(1)} %all-to-all-done.x_ref), custom_call_target="tpu_custom_call" | custom-call | flops 1207959552 | bytes 4718592 | tf_op jit(solution)/shard_map/pallas_call | solution.py:190
  52.0 2.3 %collective-permute-done.5 = bf16[4,96,256]{2,1,0:T(8,128)(2,1)S(1)} collective-permute-done((bf16[4,96,256]{2,1,0:T(8,128)(2,1)}, bf16[4,96,256]{2,1,0:T(8,128)(2,1)S(1)}, u32[]{:S(2)}, u32[]{:S(2)}) %collective-permute-start.5) | collective-permute-done | bytes 196640 | tf_op jit(solution)/shard_map/ppermute | solution.py:291
  54.3 8.5 %all-to-all-start.1 = ((bf16[16,96,256]{2,1,0:T(8,128)(2,1)}), bf16[16,96,256]{2,1,0:T(8,128)(2,1)S(1)}, u32[]{:S(2)}, u32[]{:S(2)}) async-start(bf16[16,96,256]{2,1,0:T(8,128)(2,1)} %shard_map.42), calls=%async_computation.1 | async-start | bytes 1572864 | tf_op jit(solution)/shard_map/all_to_all | solution.py:310
  62.8 2.8 %collective-permute-done.7 = bf16[4,96,256]{2,1,0:T(8,128)(2,1)S(1)} collective-permute-done((bf16[4,96,256]{2,1,0:T(8,128)(2,1)}, bf16[4,96,256]{2,1,0:T(8,128)(2,1)S(1)}, u32[]{:S(2)}, u32[]{:S(2)}) %collective-permute-start.7) | collective-permute-done | bytes 196640 | tf_op jit(solution)/shard_map/ppermute | solution.py:291
  65.5 0.1 pad_maximum_fusion.1
  65.7 0.8 collective-permute-start.8
  66.5 15.2 %collective-permute-done.8 = bf16[4,2,96,256]{3,2,0,1:T(8,128)(2,1)S(1)} collective-permute-done((bf16[4,2,96,256]{3,2,0,1:T(8,128)(2,1)S(1)}, bf16[4,2,96,256]{3,2,0,1:T(8,128)(2,1)S(1)}, u32[]{:S(2)}, u32[]{:S(2)}) %collective-permute-start.8) | collective-permute-done | bytes 393248 | tf_op jit(solution)/shard_map/ppermute | solution.py:291
  81.7 0.1 pad_maximum_fusion.2
  81.8 1.2 %collective-permute-start.9 = (bf16[8,96,256]{2,1,0:T(8,128)(2,1)S(1)}, bf16[8,96,256]{2,1,0:T(8,128)(2,1)S(1)}, u32[]{:S(2)}, u32[]{:S(2)}) collective-permute-start(bf16[8,96,256]{2,1,0:T(8,128)(2,1)S(1)} %bitcast.53), channel_id=1, source_target_pairs={{0,1},{1,0},{2,3},{3,2},{4,5},{5,4},{6,7},{7,6},{8,9},{9,8},{10,11... | collective-permute-start | bytes 1179656 | tf_op jit(solution)/shard_map/ppermute | solution.py:291
  83.0 0.8 shard_map.37.band_ref
  83.8 0.6 collective-permute-done.9.refs_1_
  84.4 1.4 %shard_map.43._ = bf16[32,96,256]{2,1,0:T(8,128)(2,1)} custom-call(s32[1]{0:T(128)} %bitcast.2.me_ref, bf16[256,256]{1,0:T(8,128)(2,1)S(1)} %shard_map.37.band_ref, bf16[8,96,256]{2,1,0:T(8,128)(2,1)S(1)} %bitcast.48, bf16[8,96,256]{2,1,0:T(8,128)(2,1)S(1)} %collective-permute-done.9.refs_1_), custom_call_target="tpu_custom_call" | custom-call | tf_op jit(solution)/shard_map/pallas_call | solution.py:277
  85.7 1.3 %shard_map.44 = bf16[32,96,256]{2,1,0:T(8,128)(2,1)} custom-call(bf16[256,256]{1,0:T(8,128)(2,1)S(1)} %shard_map.37.band_ref, bf16[16,96,256]{2,1,0:T(8,128)(2,1)S(1)} %all-to-all-done.1.x_ref, bf16[32,96,256]{2,1,0:T(8,128)(2,1)} %shard_map.43._), custom_call_target="tpu_custom_call", output_to_operand_aliasing={{}: (2, {})} | custom-call | tf_op jit(solution)/shard_map/pallas_call | solution.py:244
  (15 shorter events, 0.1 us)
Async XLA Ops:
  0.0 42.2 %copy-start = (bf16[32,1536]{1,0:T(8,128)(2,1)S(1)}, bf16[32,1536]{1,0:T(8,128)(2,1)}, u32[]{:S(2)}) copy-start(bf16[32,1536]{1,0:T(8,128)(2,1)} %param.4) | copy-start | bytes 294916
  0.0 1.4 %copy-start.1 = (bf16[32,96,256]{2,1,0:T(8,128)(2,1)S(1)}, bf16[32,96,256]{2,1,0:T(8,128)(2,1)}, u32[]{:S(2)}) copy-start(bf16[32,96,256]{2,1,0:T(8,128)(2,1)} %x_ref.3) | copy-start | bytes 4718596
  2.6 8.9 %collective-permute-start = (bf16[4,96,256]{2,1,0:T(8,128)(2,1)S(1)}, bf16[4,96,256]{2,1,0:T(8,128)(2,1)S(1)}, u32[]{:S(2)}, u32[]{:S(2)}) collective-permute-start(bf16[4,96,256]{2,1,0:T(8,128)(2,1)S(1)} %get-tuple-element.22), channel_id=1, source_target_pairs={{0,12},{1,13},{2,14},{3,15},{4,8},{5,9},{6,10},{7,11},{8,4},{9,5},... | collective-permute-start | bytes 589832 | tf_op jit(solution)/shard_map/ppermute | solution.py:291
  6.8 14.5 %collective-permute-start.1 = (bf16[4,96,256]{2,1,0:T(8,128)(2,1)S(1)}, bf16[4,96,256]{2,1,0:T(8,128)(2,1)S(1)}, u32[]{:S(2)}, u32[]{:S(2)}) collective-permute-start(bf16[4,96,256]{2,1,0:T(8,128)(2,1)S(1)} %get-tuple-element.25), channel_id=1, source_target_pairs={{0,4},{1,5},{2,6},{3,7},{4,0},{5,1},{6,2},{7,3},{8,12},{9,13},{10,... | collective-permute-start | bytes 589832 | tf_op jit(solution)/shard_map/ppermute | solution.py:291
  6.8 16.3 %collective-permute-start.2 = (bf16[4,96,256]{2,1,0:T(8,128)(2,1)S(1)}, bf16[4,96,256]{2,1,0:T(8,128)(2,1)S(1)}, u32[]{:S(2)}, u32[]{:S(2)}) collective-permute-start(bf16[4,96,256]{2,1,0:T(8,128)(2,1)S(1)} %get-tuple-element.26), channel_id=1, source_target_pairs={{0,8},{1,9},{2,10},{3,11},{4,12},{5,13},{6,14},{7,15},{8,0},{9,1},... | collective-permute-start | bytes 589832 | tf_op jit(solution)/shard_map/ppermute | solution.py:291
  11.5 38.1 %all-to-all-start = ((bf16[16,96,256]{2,1,0:T(8,128)(2,1)}), bf16[16,96,256]{2,1,0:T(8,128)(2,1)S(1)}, u32[]{:S(2)}, u32[]{:S(2)}) async-start(bf16[16,96,256]{2,1,0:T(8,128)(2,1)} %shard_map.39), calls=%async_computation | async-start | bytes 1572864 | tf_op jit(solution)/shard_map/all_to_all | solution.py:310
  23.3 17.2 %collective-permute-start.3 = (bf16[4,2,96,256]{3,2,0,1:T(8,128)(2,1)S(1)}, bf16[4,2,96,256]{3,2,0,1:T(8,128)(2,1)S(1)}, u32[]{:S(2)}, u32[]{:S(2)}) collective-permute-start(bf16[4,2,96,256]{3,2,0,1:T(8,128)(2,1)S(1)} %get-tuple-element.45), channel_id=1, source_target_pairs={{0,2},{1,3},{2,0},{3,1},{4,6},{5,7},{6,4},{7,5},{8,10},{9,11},{10,... | collective-permute-start | bytes 1179656 | tf_op jit(solution)/shard_map/ppermute | solution.py:291
  41.4 2.4 %collective-permute-start.4 = (bf16[8,96,256]{2,1,0:T(8,128)(2,1)}, bf16[8,96,256]{2,1,0:T(8,128)(2,1)S(1)}, u32[]{:S(2)}, u32[]{:S(2)}) collective-permute-start(bf16[8,96,256]{2,1,0:T(8,128)(2,1)} %bitcast.16), channel_id=1, source_target_pairs={{0,1},{1,0},{2,3},{3,2},{4,5},{5,4},{6,7},{7,6},{8,9},{9,8},{10,11... | collective-permute-start | bytes 1179656 | tf_op jit(solution)/shard_map/ppermute | solution.py:291
  46.1 8.2 %collective-permute-start.5 = (bf16[4,96,256]{2,1,0:T(8,128)(2,1)}, bf16[4,96,256]{2,1,0:T(8,128)(2,1)S(1)}, u32[]{:S(2)}, u32[]{:S(2)}) collective-permute-start(bf16[4,96,256]{2,1,0:T(8,128)(2,1)} %get-tuple-element.29), channel_id=1, source_target_pairs={{0,12},{1,13},{2,14},{3,15},{4,8},{5,9},{6,10},{7,11},{8,4},{9,5},... | collective-permute-start | bytes 589832 | tf_op jit(solution)/shard_map/ppermute | solution.py:291
  49.1 13.7 %collective-permute-start.6 = (bf16[4,96,256]{2,1,0:T(8,128)(2,1)}, bf16[4,96,256]{2,1,0:T(8,128)(2,1)S(1)}, u32[]{:S(2)}, u32[]{:S(2)}) collective-permute-start(bf16[4,96,256]{2,1,0:T(8,128)(2,1)} %get-tuple-element.31), channel_id=1, source_target_pairs={{0,4},{1,5},{2,6},{3,7},{4,0},{5,1},{6,2},{7,3},{8,12},{9,13},{10,... | collective-permute-start | bytes 589832 | tf_op jit(solution)/shard_map/ppermute | solution.py:291
  49.1 16.4 %collective-permute-start.7 = (bf16[4,96,256]{2,1,0:T(8,128)(2,1)}, bf16[4,96,256]{2,1,0:T(8,128)(2,1)S(1)}, u32[]{:S(2)}, u32[]{:S(2)}) collective-permute-start(bf16[4,96,256]{2,1,0:T(8,128)(2,1)} %get-tuple-element.32), channel_id=1, source_target_pairs={{0,8},{1,9},{2,10},{3,11},{4,12},{5,13},{6,14},{7,15},{8,0},{9,1},... | collective-permute-start | bytes 589832 | tf_op jit(solution)/shard_map/ppermute | solution.py:291
  54.3 31.5 %all-to-all-start.1 = ((bf16[16,96,256]{2,1,0:T(8,128)(2,1)}), bf16[16,96,256]{2,1,0:T(8,128)(2,1)S(1)}, u32[]{:S(2)}, u32[]{:S(2)}) async-start(bf16[16,96,256]{2,1,0:T(8,128)(2,1)} %shard_map.42), calls=%async_computation.1 | async-start | bytes 1572864 | tf_op jit(solution)/shard_map/all_to_all | solution.py:310
  65.6 17.4 %copy-start.2 = (bf16[15]{0:T(256)(128)(2,1)S(1)}, bf16[15]{0:T(256)(128)(2,1)}, u32[]{:S(2)}) copy-start(bf16[15]{0:T(256)(128)(2,1)} %param.5) | copy-start | bytes 94
  65.7 16.0 %collective-permute-start.8 = (bf16[4,2,96,256]{3,2,0,1:T(8,128)(2,1)S(1)}, bf16[4,2,96,256]{3,2,0,1:T(8,128)(2,1)S(1)}, u32[]{:S(2)}, u32[]{:S(2)}) collective-permute-start(bf16[4,2,96,256]{3,2,0,1:T(8,128)(2,1)S(1)} %get-tuple-element.41), channel_id=1, source_target_pairs={{0,2},{1,3},{2,0},{3,1},{4,6},{5,7},{6,4},{7,5},{8,10},{9,11},{10,... | collective-permute-start | bytes 1179656 | tf_op jit(solution)/shard_map/ppermute | solution.py:291
  81.8 2.5 %collective-permute-start.9 = (bf16[8,96,256]{2,1,0:T(8,128)(2,1)S(1)}, bf16[8,96,256]{2,1,0:T(8,128)(2,1)S(1)}, u32[]{:S(2)}, u32[]{:S(2)}) collective-permute-start(bf16[8,96,256]{2,1,0:T(8,128)(2,1)S(1)} %bitcast.53), channel_id=1, source_target_pairs={{0,1},{1,0},{2,3},{3,2},{4,5},{5,4},{6,7},{7,6},{8,9},{9,8},{10,11... | collective-permute-start | bytes 1179656 | tf_op jit(solution)/shard_map/ppermute | solution.py:291

commit v2 on v1

--- a/solution.py
+++ b/solution.py
@@ -232,28 +232,27 @@
     )(me, circ, *blocks)
 
 
-def vertical_first_kernel(band_ref, x_ref, _, o_ref):
+def vertical_first_kernel(band_ref, x_ref, o_ref):
     x = x_ref[...].reshape(-1, x_ref.shape[2])
     mixed = jnp.dot(x, band_ref[...], preferred_element_type=jnp.float32)
     o_ref[...] = mixed.astype(jnp.bfloat16).reshape(o_ref.shape)
 
 
-def vertical_first(band, x, result):
+def vertical_first(band, x):
     parts, count, columns = x.shape
     rows = parts // STEPS
     return pl.pallas_call(
         vertical_first_kernel,
         grid=(STEPS,),
-        in_specs=[VMEM, pl.BlockSpec((rows, count, columns), lambda i: (i, 0, 0)), HBM],
+        in_specs=[VMEM, pl.BlockSpec((rows, count, columns), lambda i: (i, 0, 0))],
         out_specs=pl.BlockSpec((rows, count, columns), lambda i: (i, 0, 0)),
-        out_shape=jax.ShapeDtypeStruct(result.shape, jnp.bfloat16),
-        input_output_aliases={2: 0},
-        compiler_params=PARAMS,
-    )(band, x, result)
+        out_shape=jax.ShapeDtypeStruct((2 * parts, count, columns), jnp.bfloat16),
+        compiler_params=PARAMS,
+    )(band, x)
 
 
 def vertical_second_kernel(me_ref, band_ref, *refs):
-    ins, (o_ref, mixed, sem) = refs[:2], refs[2:]
+    ins, (o_ref, mixed, sem) = refs[:2], refs[3:]
     parts, count, columns = mixed.shape
     half = parts // 2
     copies = []
@@ -272,19 +271,20 @@
         copy.wait()
 
 
-def vertical_second(me, band, blocks):
+def vertical_second(me, band, blocks, result):
     half, count, columns = blocks[0].shape
     return pl.pallas_call(
         vertical_second_kernel,
-        in_specs=[SMEM] + [VMEM] * 3,
+        in_specs=[SMEM] + [VMEM] * 3 + [HBM],
         out_specs=HBM,
         out_shape=jax.ShapeDtypeStruct((4 * half, count, columns), jnp.bfloat16),
         scratch_shapes=[
             pltpu.VMEM((2 * half, count, columns), jnp.bfloat16),
             pltpu.SemaphoreType.DMA((2 * half,)),
         ],
-        compiler_params=PARAMS,
-    )(me, band, *blocks)
+        input_output_aliases={4: 0},
+        compiler_params=PARAMS,
+    )(me, band, *blocks, result)
 
 
 def hop(x, distance, parts):
@@ -315,7 +315,7 @@
     circ = circulant(coef)
     arrays = far_hops(second_half(me, fields), parts)
     x = first_half(fields)
-    x, _ = lax.optimization_barrier((x, [arrays[3]]))
+    x, _ = lax.optimization_barrier((x, [arrays[1]]))
     mine = swapped(x)
     arrays = near_hops(arrays, parts)
     arrays = zonal_second(me, circ, arrays)
@@ -325,9 +325,8 @@
     _, *after = lax.optimization_barrier((done, *arrays))
     done, _ = lax.optimization_barrier((done, [arrays[3]]))
     back = swapped(done)
-    result = vertical_second(me, band, near_hops(after, parts))
-    back, result = lax.optimization_barrier((back, result))
-    return vertical_first(band, back, result)
+    blocks = near_hops(after, parts)
+    return vertical_second(me, band, blocks, vertical_first(band, back))
 
 
 def shards(fields, zonal_coef, vert_taps, *, parts):

time: 87.7 us -> 85.8 us (0.978)
  waiting for transfers between devices: 43 us -> 40.2 us
  starting transfers between devices: 30.6 us -> 31.9 us
    ppermute x10, starting transfers between devices: 12.3 us -> 16.8 us  [hop(): return lax.ppermute(x, 'lon', [(i, i ^ distance) for i in range(parts)])]
    all_to_all x2, starting transfers between devices: 18.3 us -> 15.1 us  [two_ways(): swapped = lambda x: lax.all_to_all(x, 'lon', 0, 0, tiled=True)]
    ppermute x10, waiting for transfers between devices: 43 us -> 40.2 us  [hop(): return lax.ppermute(x, 'lon', [(i, i ^ distance) for i in range(parts)])]
  transfers between devices with their start and end apart: 12 -> 12, of which waited for: 8 -> 6; matrix products, arithmetic and copies ran while one was open for 1% -> 1% of each run, Pallas kernels for 9% -> 9%
where the time goes in v2:
time: 85.8 us; the launch traced here: 85.5 us
  waiting for transfers between devices  40.2 us (47%)
  starting transfers between devices  31.9 us (37%)
  Pallas kernels  10.6 us (12%)
  local copies, waits for them, and re-layouts  1.59 us (2%)
  other arithmetic  1.08 us (1%)
    ppermute x10, waiting for transfers between devices, hop(): return lax.ppermute(x, 'lon', [(i, i ^ distance) for i in range(parts)])  40.2 us
    ppermute x10, starting transfers between devices, hop(): return lax.ppermute(x, 'lon', [(i, i ^ distance) for i in range(parts)])  16.8 us
    all_to_all x2, starting transfers between devices, two_ways(): swapped = lambda x: lax.all_to_all(x, 'lon', 0, 0, tiled=True)  15.1 us
    pallas_call x1, Pallas kernels, zonal_second(): pl.pallas_call(zonal_second_kernel, in_specs=[SMEM] + [VMEM] * 3, out_spe...  2.3 us
    pallas_call x1, Pallas kernels, zonal_first(): pl.pallas_call(zonal_first_kernel, in_specs=[VMEM, VMEM], out_specs=VMEM,...  2.27 us
  transfers between devices with their start and end apart: 12, of which 6 were waited for; matrix products, arithmetic and copies ran while one was open for 1% of the time, Pallas kernels for 9%

profile of v2, /device:TPU:1, one launch (start us, length us, event | category | flops | bytes accessed | tf_op | source)
XLA Modules:
  0.0 85.5 jit_solution(2723114628152132014)
XLA Ops:
  0.0 1.4 %copy-done.1 = bf16[32,96,256]{2,1,0:T(8,128)(2,1)S(1)} copy-done((bf16[32,96,256]{2,1,0:T(8,128)(2,1)S(1)}, bf16[32,96,256]{2,1,0:T(8,128)(2,1)}, u32[]{:S(2)}) %copy-start.1) | copy-done | bytes 1572888
  1.4 1.2 %shard_map.40 = (bf16[4,96,256]{2,1,0:T(8,128)(2,1)S(1)}, bf16[4,96,256]{2,1,0:T(8,128)(2,1)S(1)}, bf16[4,96,256]{2,1,0:T(8,128)(2,1)S(1)}, bf16[4,96,256]{2,1,0:T(8,128)(2,1)S(1)}) custom-call(s32[1]{0:T(128)} %bitcast.me_ref, bf16[32,96,256]{2,1,0:T(8,128)(2,1)S(1)} %copy-done.1), custom_call_target="tpu_custom_call" | custom-call | tf_op jit(solution)/shard_map/pallas_call | solution.py:159
  2.6 2.2 %collective-permute-start = (bf16[4,96,256]{2,1,0:T(8,128)(2,1)S(1)}, bf16[4,96,256]{2,1,0:T(8,128)(2,1)S(1)}, u32[]{:S(2)}, u32[]{:S(2)}) collective-permute-start(bf16[4,96,256]{2,1,0:T(8,128)(2,1)S(1)} %get-tuple-element.20), channel_id=1, source_target_pairs={{0,4},{1,5},{2,6},{3,7},{4,0},{5,1},{6,2},{7,3},{8,12},{9,13},{10,... | collective-permute-start | bytes 589832 | tf_op jit(solution)/shard_map/ppermute | solution.py:291
  4.8 2.3 %collective-permute-start.1 = (bf16[4,96,256]{2,1,0:T(8,128)(2,1)S(1)}, bf16[4,96,256]{2,1,0:T(8,128)(2,1)S(1)}, u32[]{:S(2)}, u32[]{:S(2)}) collective-permute-start(bf16[4,96,256]{2,1,0:T(8,128)(2,1)S(1)} %get-tuple-element.23), channel_id=1, source_target_pairs={{0,8},{1,9},{2,10},{3,11},{4,12},{5,13},{6,14},{7,15},{8,0},{9,1},... | collective-permute-start | bytes 589832 | tf_op jit(solution)/shard_map/ppermute | solution.py:291
  7.1 0.9 %shard_map.39 = bf16[16,96,256]{2,1,0:T(8,128)(2,1)} custom-call(bf16[32,96,256]{2,1,0:T(8,128)(2,1)S(1)} %copy-done.2), custom_call_target="tpu_custom_call" | custom-call | tf_op jit(solution)/shard_map/pallas_call | solution.py:135
  8.1 4.5 %collective-permute-done = bf16[4,96,256]{2,1,0:T(8,128)(2,1)S(1)} collective-permute-done((bf16[4,96,256]{2,1,0:T(8,128)(2,1)S(1)}, bf16[4,96,256]{2,1,0:T(8,128)(2,1)S(1)}, u32[]{:S(2)}, u32[]{:S(2)}) %collective-permute-start) | collective-permute-done | bytes 196640 | tf_op jit(solution)/shard_map/ppermute | solution.py:291
  12.6 7.0 %all-to-all-start = ((bf16[16,96,256]{2,1,0:T(8,128)(2,1)}), bf16[16,96,256]{2,1,0:T(8,128)(2,1)S(1)}, u32[]{:S(2)}, u32[]{:S(2)}) async-start(bf16[16,96,256]{2,1,0:T(8,128)(2,1)} %shard_map.39), calls=%async_computation | async-start | bytes 1572864 | tf_op jit(solution)/shard_map/all_to_all | solution.py:310
  19.6 0.2 collective-permute-done.2
  19.8 0.1 pad_maximum_fusion
  19.9 0.1 slice_bitcast_fusion.2
  20.0 1.3 %collective-permute-start.3 = (bf16[4,2,96,256]{3,2,0,1:T(8,128)(2,1)S(1)}, bf16[4,2,96,256]{3,2,0,1:T(8,128)(2,1)S(1)}, u32[]{:S(2)}, u32[]{:S(2)}) collective-permute-start(bf16[4,2,96,256]{3,2,0,1:T(8,128)(2,1)S(1)} %get-tuple-element.41), channel_id=1, source_target_pairs={{0,2},{1,3},{2,0},{3,1},{4,6},{5,7},{6,4},{7,5},{8,10},{9,11},{10,... | collective-permute-start | bytes 1179656 | tf_op jit(solution)/shard_map/ppermute | solution.py:291
  21.3 15.7 %collective-permute-done.3 = bf16[4,2,96,256]{3,2,0,1:T(8,128)(2,1)S(1)} collective-permute-done((bf16[4,2,96,256]{3,2,0,1:T(8,128)(2,1)S(1)}, bf16[4,2,96,256]{3,2,0,1:T(8,128)(2,1)S(1)}, u32[]{:S(2)}, u32[]{:S(2)}) %collective-permute-start.3) | collective-permute-done | bytes 393248 | tf_op jit(solution)/shard_map/ppermute | solution.py:291
  37.0 0.8 pad_maximum_fusion.3
  37.8 2.2 %collective-permute-start.4 = (bf16[8,96,256]{2,1,0:T(8,128)(2,1)}, bf16[8,96,256]{2,1,0:T(8,128)(2,1)S(1)}, u32[]{:S(2)}, u32[]{:S(2)}) collective-permute-start(bf16[8,96,256]{2,1,0:T(8,128)(2,1)} %bitcast.16), channel_id=1, source_target_pairs={{0,1},{1,0},{2,3},{3,2},{4,5},{5,4},{6,7},{7,6},{8,9},{9,8},{10,11... | collective-permute-start | bytes 1179656 | tf_op jit(solution)/shard_map/ppermute | solution.py:291
  40.0 0.5 shard_map.38.circ_ref
  40.5 1.0 %collective-permute-done.4.refs_1_ = bf16[8,96,256]{2,1,0:T(8,128)(2,1)S(1)} collective-permute-done((bf16[8,96,256]{2,1,0:T(8,128)(2,1)}, bf16[8,96,256]{2,1,0:T(8,128)(2,1)S(1)}, u32[]{:S(2)}, u32[]{:S(2)}) %collective-permute-start.4) | collective-permute-done | bytes 393248 | tf_op jit(solution)/shard_map/ppermute | solution.py:291
  41.5 2.3 %shard_map.41 = (bf16[4,96,256]{2,1,0:T(8,128)(2,1)S(1)}, bf16[4,96,256]{2,1,0:T(8,128)(2,1)}, bf16[4,96,256]{2,1,0:T(8,128)(2,1)}, bf16[4,96,256]{2,1,0:T(8,128)(2,1)}) custom-call(s32[1]{0:T(128)} %bitcast.me_ref, bf16[2,1536,256]{2,1,0:T(8,128)(2,1)S(1)} %shard_map.38.circ_ref, bf16[8,96,256]{2,1,0:T(8,128)(2,1)S(1)} %bitcast.49, ...), custom_call_target="tpu_custom_call" | custom-call | flops 1207959552 | bytes 4718592 | tf_op jit(solution)/shard_map/pallas_call | solution.py:224
  43.8 2.9 %collective-permute-start.7 = (bf16[4,96,256]{2,1,0:T(8,128)(2,1)}, bf16[4,96,256]{2,1,0:T(8,128)(2,1)S(1)}, u32[]{:S(2)}, u32[]{:S(2)}) collective-permute-start(bf16[4,96,256]{2,1,0:T(8,128)(2,1)} %get-tuple-element.29), channel_id=1, source_target_pairs={{0,12},{1,13},{2,14},{3,15},{4,8},{5,9},{6,10},{7,11},{8,4},{9,5},... | collective-permute-start | bytes 589832 | tf_op jit(solution)/shard_map/ppermute | solution.py:291
  46.7 4.7 %collective-permute-start.5 = (bf16[4,96,256]{2,1,0:T(8,128)(2,1)}, bf16[4,96,256]{2,1,0:T(8,128)(2,1)S(1)}, u32[]{:S(2)}, u32[]{:S(2)}) collective-permute-start(bf16[4,96,256]{2,1,0:T(8,128)(2,1)} %get-tuple-element.27), channel_id=1, source_target_pairs={{0,4},{1,5},{2,6},{3,7},{4,0},{5,1},{6,2},{7,3},{8,12},{9,13},{10,... | collective-permute-start | bytes 589832 | tf_op jit(solution)/shard_map/ppermute | solution.py:291
  51.4 2.3 %shard_map.42 = bf16[16,96,256]{2,1,0:T(8,128)(2,1)} custom-call(bf16[2,1536,256]{2,1,0:T(8,128)(2,1)S(1)} %shard_map.38.circ_ref, bf16[16,96,256]{2,1,0:T(8,128)(2,1)S(1)} %all-to-all-done.x_ref), custom_call_target="tpu_custom_call" | custom-call | flops 1207959552 | bytes 4718592 | tf_op jit(solution)/shard_map/pallas_call | solution.py:190
  53.7 8.1 %all-to-all-start.1 = ((bf16[16,96,256]{2,1,0:T(8,128)(2,1)}), bf16[16,96,256]{2,1,0:T(8,128)(2,1)S(1)}, u32[]{:S(2)}, u32[]{:S(2)}) async-start(bf16[16,96,256]{2,1,0:T(8,128)(2,1)} %shard_map.42), calls=%async_computation.1 | async-start | bytes 1572864 | tf_op jit(solution)/shard_map/all_to_all | solution.py:310
  61.8 3.2 %collective-permute-done.6 = bf16[4,96,256]{2,1,0:T(8,128)(2,1)S(1)} collective-permute-done((bf16[4,96,256]{2,1,0:T(8,128)(2,1)}, bf16[4,96,256]{2,1,0:T(8,128)(2,1)S(1)}, u32[]{:S(2)}, u32[]{:S(2)}) %collective-permute-start.6) | collective-permute-done | bytes 196640 | tf_op jit(solution)/shard_map/ppermute | solution.py:291
  65.0 0.1 pad_maximum_fusion.1
  65.1 0.0 copy-start.3
  65.1 0.1 slice_bitcast_fusion
  65.2 0.1 collective-permute-start.8
  65.3 15.6 %collective-permute-done.8 = bf16[4,2,96,256]{3,2,0,1:T(8,128)(2,1)S(1)} collective-permute-done((bf16[4,2,96,256]{3,2,0,1:T(8,128)(2,1)S(1)}, bf16[4,2,96,256]{3,2,0,1:T(8,128)(2,1)S(1)}, u32[]{:S(2)}, u32[]{:S(2)}) %collective-permute-start.8) | collective-permute-done | bytes 393248 | tf_op jit(solution)/shard_map/ppermute | solution.py:291
  80.8 0.1 pad_maximum_fusion.2
  80.9 1.1 %collective-permute-start.9 = (bf16[8,96,256]{2,1,0:T(8,128)(2,1)S(1)}, bf16[8,96,256]{2,1,0:T(8,128)(2,1)S(1)}, u32[]{:S(2)}, u32[]{:S(2)}) collective-permute-start(bf16[8,96,256]{2,1,0:T(8,128)(2,1)S(1)} %bitcast.53), channel_id=1, source_target_pairs={{0,1},{1,0},{2,3},{3,2},{4,5},{5,4},{6,7},{7,6},{8,9},{9,8},{10,11... | collective-permute-start | bytes 1179656 | tf_op jit(solution)/shard_map/ppermute | solution.py:291
  82.1 0.8 shard_map.37.band_ref
  82.8 1.3 %shard_map.43.refs_2_ = bf16[32,96,256]{2,1,0:T(8,128)(2,1)} custom-call(bf16[256,256]{1,0:T(8,128)(2,1)S(1)} %shard_map.37.band_ref, bf16[16,96,256]{2,1,0:T(8,128)(2,1)S(1)} %all-to-all-done.1.x_ref), custom_call_target="tpu_custom_call" | custom-call | tf_op jit(solution)/shard_map/pallas_call | solution.py:244
  84.1 1.4 %shard_map.44 = bf16[32,96,256]{2,1,0:T(8,128)(2,1)} custom-call(s32[1]{0:T(128)} %bitcast.me_ref, bf16[256,256]{1,0:T(8,128)(2,1)S(1)} %shard_map.37.band_ref, bf16[8,96,256]{2,1,0:T(8,128)(2,1)S(1)} %bitcast.48, bf16[8,96,256]{2,1,0:T(8,128)(2,1)S(1)} %collective-permute-done.9.refs_1_, ...), custom_call_target="tpu_custom_call", output_to_operand_aliasing={{}: (4, {})} | custom-call | tf_op jit(solution)/shard_map/pallas_call | solution.py:276
  (17 shorter events, 0.1 us)
Async XLA Ops:
  0.0 39.9 %copy-start = (bf16[32,1536]{1,0:T(8,128)(2,1)S(1)}, bf16[32,1536]{1,0:T(8,128)(2,1)}, u32[]{:S(2)}) copy-start(bf16[32,1536]{1,0:T(8,128)(2,1)} %param.4) | copy-start | bytes 294916
  0.0 1.4 %copy-start.1 = (bf16[32,96,256]{2,1,0:T(8,128)(2,1)S(1)}, bf16[32,96,256]{2,1,0:T(8,128)(2,1)}, u32[]{:S(2)}) copy-start(bf16[32,96,256]{2,1,0:T(8,128)(2,1)} %x_ref.3) | copy-start | bytes 4718596
  1.4 5.7 %copy-start.2 = (bf16[32,96,256]{2,1,0:T(8,128)(2,1)S(1)}, bf16[32,96,256]{2,1,0:T(8,128)(2,1)}, u32[]{:S(2)}) copy-start(bf16[32,96,256]{2,1,0:T(8,128)(2,1)} %x_ref.3) | copy-start | bytes 4718596
  2.6 10.0 %collective-permute-start = (bf16[4,96,256]{2,1,0:T(8,128)(2,1)S(1)}, bf16[4,96,256]{2,1,0:T(8,128)(2,1)S(1)}, u32[]{:S(2)}, u32[]{:S(2)}) collective-permute-start(bf16[4,96,256]{2,1,0:T(8,128)(2,1)S(1)} %get-tuple-element.20), channel_id=1, source_target_pairs={{0,4},{1,5},{2,6},{3,7},{4,0},{5,1},{6,2},{7,3},{8,12},{9,13},{10,... | collective-permute-start | bytes 589832 | tf_op jit(solution)/shard_map/ppermute | solution.py:291
  4.8 14.7 %collective-permute-start.1 = (bf16[4,96,256]{2,1,0:T(8,128)(2,1)S(1)}, bf16[4,96,256]{2,1,0:T(8,128)(2,1)S(1)}, u32[]{:S(2)}, u32[]{:S(2)}) collective-permute-start(bf16[4,96,256]{2,1,0:T(8,128)(2,1)S(1)} %get-tuple-element.23), channel_id=1, source_target_pairs={{0,8},{1,9},{2,10},{3,11},{4,12},{5,13},{6,14},{7,15},{8,0},{9,1},... | collective-permute-start | bytes 589832 | tf_op jit(solution)/shard_map/ppermute | solution.py:291
  7.1 12.7 %collective-permute-start.2 = (bf16[4,96,256]{2,1,0:T(8,128)(2,1)S(1)}, bf16[4,96,256]{2,1,0:T(8,128)(2,1)S(1)}, u32[]{:S(2)}, u32[]{:S(2)}) collective-permute-start(bf16[4,96,256]{2,1,0:T(8,128)(2,1)S(1)} %get-tuple-element.24), channel_id=1, source_target_pairs={{0,12},{1,13},{2,14},{3,15},{4,8},{5,9},{6,10},{7,11},{8,4},{9,5},... | collective-permute-start | bytes 589832 | tf_op jit(solution)/shard_map/ppermute | solution.py:291
  12.6 38.8 %all-to-all-start = ((bf16[16,96,256]{2,1,0:T(8,128)(2,1)}), bf16[16,96,256]{2,1,0:T(8,128)(2,1)S(1)}, u32[]{:S(2)}, u32[]{:S(2)}) async-start(bf16[16,96,256]{2,1,0:T(8,128)(2,1)} %shard_map.39), calls=%async_computation | async-start | bytes 1572864 | tf_op jit(solution)/shard_map/all_to_all | solution.py:310
  20.0 17.0 %collective-permute-start.3 = (bf16[4,2,96,256]{3,2,0,1:T(8,128)(2,1)S(1)}, bf16[4,2,96,256]{3,2,0,1:T(8,128)(2,1)S(1)}, u32[]{:S(2)}, u32[]{:S(2)}) collective-permute-start(bf16[4,2,96,256]{3,2,0,1:T(8,128)(2,1)S(1)} %get-tuple-element.41), channel_id=1, source_target_pairs={{0,2},{1,3},{2,0},{3,1},{4,6},{5,7},{6,4},{7,5},{8,10},{9,11},{10,... | collective-permute-start | bytes 1179656 | tf_op jit(solution)/shard_map/ppermute | solution.py:291
  37.8 3.7 %collective-permute-start.4 = (bf16[8,96,256]{2,1,0:T(8,128)(2,1)}, bf16[8,96,256]{2,1,0:T(8,128)(2,1)S(1)}, u32[]{:S(2)}, u32[]{:S(2)}) collective-permute-start(bf16[8,96,256]{2,1,0:T(8,128)(2,1)} %bitcast.16), channel_id=1, source_target_pairs={{0,1},{1,0},{2,3},{3,2},{4,5},{5,4},{6,7},{7,6},{8,9},{9,8},{10,11... | collective-permute-start | bytes 1179656 | tf_op jit(solution)/shard_map/ppermute | solution.py:291
  43.8 9.9 %collective-permute-start.7 = (bf16[4,96,256]{2,1,0:T(8,128)(2,1)}, bf16[4,96,256]{2,1,0:T(8,128)(2,1)S(1)}, u32[]{:S(2)}, u32[]{:S(2)}) collective-permute-start(bf16[4,96,256]{2,1,0:T(8,128)(2,1)} %get-tuple-element.29), channel_id=1, source_target_pairs={{0,12},{1,13},{2,14},{3,15},{4,8},{5,9},{6,10},{7,11},{8,4},{9,5},... | collective-permute-start | bytes 589832 | tf_op jit(solution)/shard_map/ppermute | solution.py:291
  46.7 15.1 %collective-permute-start.5 = (bf16[4,96,256]{2,1,0:T(8,128)(2,1)}, bf16[4,96,256]{2,1,0:T(8,128)(2,1)S(1)}, u32[]{:S(2)}, u32[]{:S(2)}) collective-permute-start(bf16[4,96,256]{2,1,0:T(8,128)(2,1)} %get-tuple-element.27), channel_id=1, source_target_pairs={{0,4},{1,5},{2,6},{3,7},{4,0},{5,1},{6,2},{7,3},{8,12},{9,13},{10,... | collective-permute-start | bytes 589832 | tf_op jit(solution)/shard_map/ppermute | solution.py:291
  51.4 13.6 %collective-permute-start.6 = (bf16[4,96,256]{2,1,0:T(8,128)(2,1)}, bf16[4,96,256]{2,1,0:T(8,128)(2,1)S(1)}, u32[]{:S(2)}, u32[]{:S(2)}) collective-permute-start(bf16[4,96,256]{2,1,0:T(8,128)(2,1)} %get-tuple-element.28), channel_id=1, source_target_pairs={{0,8},{1,9},{2,10},{3,11},{4,12},{5,13},{6,14},{7,15},{8,0},{9,1},... | collective-permute-start | bytes 589832 | tf_op jit(solution)/shard_map/ppermute | solution.py:291
  53.7 29.1 %all-to-all-start.1 = ((bf16[16,96,256]{2,1,0:T(8,128)(2,1)}), bf16[16,96,256]{2,1,0:T(8,128)(2,1)S(1)}, u32[]{:S(2)}, u32[]{:S(2)}) async-start(bf16[16,96,256]{2,1,0:T(8,128)(2,1)} %shard_map.42), calls=%async_computation.1 | async-start | bytes 1572864 | tf_op jit(solution)/shard_map/all_to_all | solution.py:310
  65.1 16.9 %copy-start.3 = (bf16[15]{0:T(256)(128)(2,1)S(1)}, bf16[15]{0:T(256)(128)(2,1)}, u32[]{:S(2)}) copy-start(bf16[15]{0:T(256)(128)(2,1)} %param.5) | copy-start | bytes 94
  65.2 15.6 %collective-permute-start.8 = (bf16[4,2,96,256]{3,2,0,1:T(8,128)(2,1)S(1)}, bf16[4,2,96,256]{3,2,0,1:T(8,128)(2,1)S(1)}, u32[]{:S(2)}, u32[]{:S(2)}) collective-permute-start(bf16[4,2,96,256]{3,2,0,1:T(8,128)(2,1)S(1)} %get-tuple-element.37), channel_id=1, source_target_pairs={{0,2},{1,3},{2,0},{3,1},{4,6},{5,7},{6,4},{7,5},{8,10},{9,11},{10,... | collective-permute-start | bytes 1179656 | tf_op jit(solution)/shard_map/ppermute | solution.py:291
  80.9 3.2 %collective-permute-start.9 = (bf16[8,96,256]{2,1,0:T(8,128)(2,1)S(1)}, bf16[8,96,256]{2,1,0:T(8,128)(2,1)S(1)}, u32[]{:S(2)}, u32[]{:S(2)}) collective-permute-start(bf16[8,96,256]{2,1,0:T(8,128)(2,1)S(1)} %bitcast.53), channel_id=1, source_target_pairs={{0,1},{1,0},{2,3},{3,2},{4,5},{5,4},{6,7},{7,6},{8,9},{9,8},{10,11... | collective-permute-start | bytes 1179656 | tf_op jit(solution)/shard_map/ppermute | solution.py:291

commit v3 on v2

--- a/solution.py
+++ b/solution.py
@@ -138,31 +138,30 @@
         out_specs=VMEM,
         out_shape=jax.ShapeDtypeStruct((lat_rows // 2, count, columns), jnp.bfloat16),
         scratch_shapes=[pltpu.SemaphoreType.DMA((1,))],
-        compiler_params=PARAMS,
+        compiler_params=pltpu.CompilerParams(vmem_limit_bytes=61 * 1024 * 1024),
     )(x)
 
 
-def second_half_kernel(me_ref, x_ref, *refs):
+def second_half_kernel(first, me_ref, x_ref, *refs):
     outs, sem = refs[:-1], refs[-1]
-    half = len(outs) * NEAR
+    half = x_ref.shape[0] // 2
     copies = []
-    for r in range(half):
-        x = x_ref.at[half + (me_ref[0] ^ r)]
-        out = outs[r // NEAR].at[r % NEAR]
-        copies.append(pltpu.make_async_copy(x, out, sem.at[r]))
+    for i in range(len(outs) * NEAR):
+        x = x_ref.at[half + (me_ref[0] ^ (first * NEAR + i))]
+        out = outs[i // NEAR].at[i % NEAR]
+        copies.append(pltpu.make_async_copy(x, out, sem.at[i]))
     copied(copies)
 
 
-def second_half(me, x):
-    lat_rows, count, columns = x.shape
-    arrays = lat_rows // 2 // NEAR
-    return pl.pallas_call(
-        second_half_kernel,
+def second_half(me, x, first, arrays):
+    _, count, columns = x.shape
+    return pl.pallas_call(
+        functools.partial(second_half_kernel, first),
         in_specs=[SMEM, HBM],
         out_specs=[VMEM] * arrays,
         out_shape=[jax.ShapeDtypeStruct((NEAR, count, columns), jnp.bfloat16)] * arrays,
-        scratch_shapes=[pltpu.SemaphoreType.DMA((lat_rows // 2,))],
-        compiler_params=PARAMS,
+        scratch_shapes=[pltpu.SemaphoreType.DMA((arrays * NEAR,))],
+        compiler_params=pltpu.CompilerParams(vmem_limit_bytes=61 * 1024 * 1024),
     )(me, x)
 
 
@@ -179,10 +178,10 @@
     o_ref[...] = total.astype(jnp.bfloat16).reshape(o_ref.shape)
 
 
-def zonal_cost(circ, columns):
+def zonal_cost(circ, columns, times=1):
     n = circ.shape[1]
     return pl.CostEstimate(
-        flops=2 * n * n * columns, bytes_accessed=2 * n * n, transcendentals=0
+        flops=int(times * 2 * n * n * columns), bytes_accessed=2 * n * n, transcendentals=0
     )
 
 
@@ -228,7 +227,7 @@
         out_shape=[jax.ShapeDtypeStruct((NEAR, count, columns), jnp.bfloat16)] * arrays,
         scratch_shapes=[pltpu.VMEM((2 * half, count, columns), jnp.bfloat16)] * 2,
         compiler_params=PARAMS,
-        cost_estimate=zonal_cost(circ, columns),
+        cost_estimate=zonal_cost(circ, columns, 4),
     )(me, circ, *blocks)
 
 
@@ -313,7 +312,9 @@
         zonal_coef.reshape(2, parts, -1), position, 1, keepdims=False
     )
     circ = circulant(coef)
-    arrays = far_hops(second_half(me, fields), parts)
+    far = second_half(me, fields, 1, parts // NEAR - 1)
+    stays, _ = lax.optimization_barrier((fields, far[0]))
+    arrays = far_hops([*second_half(me, stays, 0, 1), *far], parts)
     x = first_half(fields)
     x, _ = lax.optimization_barrier((x, [arrays[1]]))
     mine = swapped(x)

time: 85.8 us -> 85.6 us (level)
  Pallas kernels: 10.6 us -> 14.1 us
  waiting for transfers between devices: 40.2 us -> 37.6 us
  local copies, waits for them, and re-layouts: 1.59 us -> 0.16 us
    ppermute x10, waiting for transfers between devices: 40.2 us -> 37.6 us  [hop(): return lax.ppermute(x, 'lon', [(i, i ^ distance) for i in range(parts)])]
    pallas_call x1 -> x2, Pallas kernels: 1.18 us -> 3.6 us  [second_half(): pl.pallas_call(functools.partial(second_half_kernel, first), in_specs=[SM...]
    unnamed x9 -> x7, local copies, waits for them, and re-layouts: 1.46 us -> 0.02 us
    pallas_call x1, Pallas kernels: 0.94 us -> 2.02 us  [first_half(): pl.pallas_call(first_half_kernel, in_specs=[HBM], out_specs=VMEM, out_sha...]
  transfers between devices with their start and end apart: 12 -> 12, of which waited for: 6 -> 6; matrix products, arithmetic and copies ran while one was open for 1% -> 1% of each run, Pallas kernels for 9% -> 13%
where the time goes in v3:
time: 85.6 us; the launch traced here: 85.1 us
  waiting for transfers between devices  37.6 us (44%)
  starting transfers between devices  32 us (37%)
  Pallas kernels  14.1 us (16%)
  other arithmetic  1.09 us (1%)
    ppermute x10, waiting for transfers between devices, hop(): return lax.ppermute(x, 'lon', [(i, i ^ distance) for i in range(parts)])  37.6 us
    ppermute x10, starting transfers between devices, hop(): return lax.ppermute(x, 'lon', [(i, i ^ distance) for i in range(parts)])  16.9 us
    all_to_all x2, starting transfers between devices, two_ways(): swapped = lambda x: lax.all_to_all(x, 'lon', 0, 0, tiled=True)  15.1 us
    pallas_call x2, Pallas kernels, second_half(): pl.pallas_call(functools.partial(second_half_kernel, first), in_specs=[SM...  3.6 us
    pallas_call x1, Pallas kernels, zonal_second(): pl.pallas_call(zonal_second_kernel, in_specs=[SMEM] + [VMEM] * 3, out_spe...  2.29 us
    pallas_call x1, Pallas kernels, zonal_first(): pl.pallas_call(zonal_first_kernel, in_specs=[VMEM, VMEM], out_specs=VMEM,...  2.28 us
    pallas_call x1, Pallas kernels, first_half(): pl.pallas_call(first_half_kernel, in_specs=[HBM], out_specs=VMEM, out_sha...  2.02 us
  transfers between devices with their start and end apart: 12, of which 6 were waited for; matrix products, arithmetic and copies ran while one was open for 1% of the time, Pallas kernels for 13%

profile of v3, /device:TPU:1, one launch (start us, length us, event | category | flops | bytes accessed | tf_op | source)
XLA Modules:
  0.0 85.1 jit_solution(5255393262443949323)
XLA Ops:
  0.0 2.0 %shard_map.40 = (bf16[4,96,256]{2,1,0:T(8,128)(2,1)}, bf16[4,96,256]{2,1,0:T(8,128)(2,1)}, bf16[4,96,256]{2,1,0:T(8,128)(2,1)}) custom-call(s32[1]{0:T(128)} %bitcast.me_ref, bf16[32,96,256]{2,1,0:T(8,128)(2,1)} %x_ref.4), custom_call_target="tpu_custom_call" | custom-call | tf_op jit(solution)/shard_map/pallas_call | solution.py:158
  2.0 2.2 %collective-permute-start = (bf16[4,96,256]{2,1,0:T(8,128)(2,1)}, bf16[4,96,256]{2,1,0:T(8,128)(2,1)S(1)}, u32[]{:S(2)}, u32[]{:S(2)}) collective-permute-start(bf16[4,96,256]{2,1,0:T(8,128)(2,1)} %get-tuple-element.20), channel_id=1, source_target_pairs={{0,4},{1,5},{2,6},{3,7},{4,0},{5,1},{6,2},{7,3},{8,12},{9,13},{10,... | collective-permute-start | bytes 589832 | tf_op jit(solution)/shard_map/ppermute | solution.py:290
  4.2 2.3 %collective-permute-start.1 = (bf16[4,96,256]{2,1,0:T(8,128)(2,1)}, bf16[4,96,256]{2,1,0:T(8,128)(2,1)S(1)}, u32[]{:S(2)}, u32[]{:S(2)}) collective-permute-start(bf16[4,96,256]{2,1,0:T(8,128)(2,1)} %get-tuple-element.23), channel_id=1, source_target_pairs={{0,8},{1,9},{2,10},{3,11},{4,12},{5,13},{6,14},{7,15},{8,0},{9,1},... | collective-permute-start | bytes 589832 | tf_op jit(solution)/shard_map/ppermute | solution.py:290
  6.5 2.0 %shard_map.39 = bf16[16,96,256]{2,1,0:T(8,128)(2,1)} custom-call(bf16[32,96,256]{2,1,0:T(8,128)(2,1)} %x_ref.4), custom_call_target="tpu_custom_call" | custom-call | tf_op jit(solution)/shard_map/pallas_call | solution.py:135
  8.6 1.6 %shard_map.41 = bf16[4,96,256]{2,1,0:T(8,128)(2,1)} custom-call(s32[1]{0:T(128)} %bitcast.me_ref, bf16[32,96,256]{2,1,0:T(8,128)(2,1)} %x_ref.4), custom_call_target="tpu_custom_call" | custom-call | tf_op jit(solution)/shard_map/pallas_call | solution.py:158
  10.2 2.0 %collective-permute-done = bf16[4,96,256]{2,1,0:T(8,128)(2,1)S(1)} collective-permute-done((bf16[4,96,256]{2,1,0:T(8,128)(2,1)}, bf16[4,96,256]{2,1,0:T(8,128)(2,1)S(1)}, u32[]{:S(2)}, u32[]{:S(2)}) %collective-permute-start) | collective-permute-done | bytes 196640 | tf_op jit(solution)/shard_map/ppermute | solution.py:290
  12.2 7.0 %all-to-all-start = ((bf16[16,96,256]{2,1,0:T(8,128)(2,1)}), bf16[16,96,256]{2,1,0:T(8,128)(2,1)S(1)}, u32[]{:S(2)}, u32[]{:S(2)}) async-start(bf16[16,96,256]{2,1,0:T(8,128)(2,1)} %shard_map.39), calls=%async_computation | async-start | bytes 1572864 | tf_op jit(solution)/shard_map/all_to_all | solution.py:309
  19.2 0.2 collective-permute-done.2
  19.4 0.1 pad_maximum_fusion
  19.5 0.1 slice_bitcast_fusion.2
  19.6 1.3 %collective-permute-start.3 = (bf16[4,2,96,256]{3,2,0,1:T(8,128)(2,1)S(1)}, bf16[4,2,96,256]{3,2,0,1:T(8,128)(2,1)S(1)}, u32[]{:S(2)}, u32[]{:S(2)}) collective-permute-start(bf16[4,2,96,256]{3,2,0,1:T(8,128)(2,1)S(1)} %get-tuple-element.41), channel_id=1, source_target_pairs={{0,2},{1,3},{2,0},{3,1},{4,6},{5,7},{6,4},{7,5},{8,10},{9,11},{10,... | collective-permute-start | bytes 1179656 | tf_op jit(solution)/shard_map/ppermute | solution.py:290
  20.9 15.6 %collective-permute-done.3 = bf16[4,2,96,256]{3,2,0,1:T(8,128)(2,1)S(1)} collective-permute-done((bf16[4,2,96,256]{3,2,0,1:T(8,128)(2,1)S(1)}, bf16[4,2,96,256]{3,2,0,1:T(8,128)(2,1)S(1)}, u32[]{:S(2)}, u32[]{:S(2)}) %collective-permute-start.3) | collective-permute-done | bytes 393248 | tf_op jit(solution)/shard_map/ppermute | solution.py:290
  36.5 0.8 pad_maximum_fusion.3
  37.3 2.2 %collective-permute-start.4 = (bf16[8,96,256]{2,1,0:T(8,128)(2,1)}, bf16[8,96,256]{2,1,0:T(8,128)(2,1)S(1)}, u32[]{:S(2)}, u32[]{:S(2)}) collective-permute-start(bf16[8,96,256]{2,1,0:T(8,128)(2,1)} %bitcast.16), channel_id=1, source_target_pairs={{0,1},{1,0},{2,3},{3,2},{4,5},{5,4},{6,7},{7,6},{8,9},{9,8},{10,11... | collective-permute-start | bytes 1179656 | tf_op jit(solution)/shard_map/ppermute | solution.py:290
  39.6 0.5 shard_map.38.circ_ref
  40.1 1.0 %collective-permute-done.4.refs_1_ = bf16[8,96,256]{2,1,0:T(8,128)(2,1)S(1)} collective-permute-done((bf16[8,96,256]{2,1,0:T(8,128)(2,1)}, bf16[8,96,256]{2,1,0:T(8,128)(2,1)S(1)}, u32[]{:S(2)}, u32[]{:S(2)}) %collective-permute-start.4) | collective-permute-done | bytes 393248 | tf_op jit(solution)/shard_map/ppermute | solution.py:290
  41.1 2.3 %shard_map.42 = (bf16[4,96,256]{2,1,0:T(8,128)(2,1)S(1)}, bf16[4,96,256]{2,1,0:T(8,128)(2,1)}, bf16[4,96,256]{2,1,0:T(8,128)(2,1)}, bf16[4,96,256]{2,1,0:T(8,128)(2,1)}) custom-call(s32[1]{0:T(128)} %bitcast.me_ref, bf16[2,1536,256]{2,1,0:T(8,128)(2,1)S(1)} %shard_map.38.circ_ref, bf16[8,96,256]{2,1,0:T(8,128)(2,1)S(1)} %bitcast.49, ...), custom_call_target="tpu_custom_call" | custom-call | flops 4831838208 | bytes 4718592 | tf_op jit(solution)/shard_map/pallas_call | solution.py:223
  43.4 2.9 %collective-permute-start.7 = (bf16[4,96,256]{2,1,0:T(8,128)(2,1)}, bf16[4,96,256]{2,1,0:T(8,128)(2,1)S(1)}, u32[]{:S(2)}, u32[]{:S(2)}) collective-permute-start(bf16[4,96,256]{2,1,0:T(8,128)(2,1)} %get-tuple-element.29), channel_id=1, source_target_pairs={{0,12},{1,13},{2,14},{3,15},{4,8},{5,9},{6,10},{7,11},{8,4},{9,5},... | collective-permute-start | bytes 589832 | tf_op jit(solution)/shard_map/ppermute | solution.py:290
  46.3 4.7 %collective-permute-start.5 = (bf16[4,96,256]{2,1,0:T(8,128)(2,1)}, bf16[4,96,256]{2,1,0:T(8,128)(2,1)S(1)}, u32[]{:S(2)}, u32[]{:S(2)}) collective-permute-start(bf16[4,96,256]{2,1,0:T(8,128)(2,1)} %get-tuple-element.27), channel_id=1, source_target_pairs={{0,4},{1,5},{2,6},{3,7},{4,0},{5,1},{6,2},{7,3},{8,12},{9,13},{10,... | collective-permute-start | bytes 589832 | tf_op jit(solution)/shard_map/ppermute | solution.py:290
  51.0 2.3 %shard_map.43 = bf16[16,96,256]{2,1,0:T(8,128)(2,1)} custom-call(bf16[2,1536,256]{2,1,0:T(8,128)(2,1)S(1)} %shard_map.38.circ_ref, bf16[16,96,256]{2,1,0:T(8,128)(2,1)S(1)} %all-to-all-done.x_ref), custom_call_target="tpu_custom_call" | custom-call | flops 1207959552 | bytes 4718592 | tf_op jit(solution)/shard_map/pallas_call | solution.py:189
  53.3 8.1 %all-to-all-start.1 = ((bf16[16,96,256]{2,1,0:T(8,128)(2,1)}), bf16[16,96,256]{2,1,0:T(8,128)(2,1)S(1)}, u32[]{:S(2)}, u32[]{:S(2)}) async-start(bf16[16,96,256]{2,1,0:T(8,128)(2,1)} %shard_map.43), calls=%async_computation.1 | async-start | bytes 1572864 | tf_op jit(solution)/shard_map/all_to_all | solution.py:309
  61.5 3.1 %collective-permute-done.6 = bf16[4,96,256]{2,1,0:T(8,128)(2,1)S(1)} collective-permute-done((bf16[4,96,256]{2,1,0:T(8,128)(2,1)}, bf16[4,96,256]{2,1,0:T(8,128)(2,1)S(1)}, u32[]{:S(2)}, u32[]{:S(2)}) %collective-permute-start.6) | collective-permute-done | bytes 196640 | tf_op jit(solution)/shard_map/ppermute | solution.py:290
  64.6 0.1 pad_maximum_fusion.1
  64.7 0.0 copy-start.2
  64.7 0.1 slice_bitcast_fusion
  64.8 0.1 collective-permute-start.8
  64.9 15.6 %collective-permute-done.8 = bf16[4,2,96,256]{3,2,0,1:T(8,128)(2,1)S(1)} collective-permute-done((bf16[4,2,96,256]{3,2,0,1:T(8,128)(2,1)S(1)}, bf16[4,2,96,256]{3,2,0,1:T(8,128)(2,1)S(1)}, u32[]{:S(2)}, u32[]{:S(2)}) %collective-permute-start.8) | collective-permute-done | bytes 393248 | tf_op jit(solution)/shard_map/ppermute | solution.py:290
  80.5 0.1 pad_maximum_fusion.2
  80.6 1.1 %collective-permute-start.9 = (bf16[8,96,256]{2,1,0:T(8,128)(2,1)S(1)}, bf16[8,96,256]{2,1,0:T(8,128)(2,1)S(1)}, u32[]{:S(2)}, u32[]{:S(2)}) collective-permute-start(bf16[8,96,256]{2,1,0:T(8,128)(2,1)S(1)} %bitcast.53), channel_id=1, source_target_pairs={{0,1},{1,0},{2,3},{3,2},{4,5},{5,4},{6,7},{7,6},{8,9},{9,8},{10,11... | collective-permute-start | bytes 1179656 | tf_op jit(solution)/shard_map/ppermute | solution.py:290
  81.7 0.8 shard_map.37.band_ref
  82.5 1.3 %shard_map.44.refs_2_ = bf16[32,96,256]{2,1,0:T(8,128)(2,1)} custom-call(bf16[256,256]{1,0:T(8,128)(2,1)S(1)} %shard_map.37.band_ref, bf16[16,96,256]{2,1,0:T(8,128)(2,1)S(1)} %all-to-all-done.1.x_ref), custom_call_target="tpu_custom_call" | custom-call | tf_op jit(solution)/shard_map/pallas_call | solution.py:243
  83.8 1.4 %shard_map.45 = bf16[32,96,256]{2,1,0:T(8,128)(2,1)} custom-call(s32[1]{0:T(128)} %bitcast.me_ref, bf16[256,256]{1,0:T(8,128)(2,1)S(1)} %shard_map.37.band_ref, bf16[8,96,256]{2,1,0:T(8,128)(2,1)S(1)} %bitcast.48, bf16[8,96,256]{2,1,0:T(8,128)(2,1)S(1)} %collective-permute-done.9.refs_1_, ...), custom_call_target="tpu_custom_call", output_to_operand_aliasing={{}: (4, {})} | custom-call | tf_op jit(solution)/shard_map/pallas_call | solution.py:275
  (16 shorter events, 0.1 us)
Async XLA Ops:
  0.0 39.6 %copy-start = (bf16[32,1536]{1,0:T(8,128)(2,1)S(1)}, bf16[32,1536]{1,0:T(8,128)(2,1)}, u32[]{:S(2)}) copy-start(bf16[32,1536]{1,0:T(8,128)(2,1)} %param.4) | copy-start | bytes 294916
  2.0 10.2 %collective-permute-start = (bf16[4,96,256]{2,1,0:T(8,128)(2,1)}, bf16[4,96,256]{2,1,0:T(8,128)(2,1)S(1)}, u32[]{:S(2)}, u32[]{:S(2)}) collective-permute-start(bf16[4,96,256]{2,1,0:T(8,128)(2,1)} %get-tuple-element.20), channel_id=1, source_target_pairs={{0,4},{1,5},{2,6},{3,7},{4,0},{5,1},{6,2},{7,3},{8,12},{9,13},{10,... | collective-permute-start | bytes 589832 | tf_op jit(solution)/shard_map/ppermute | solution.py:290
  4.2 15.0 %collective-permute-start.1 = (bf16[4,96,256]{2,1,0:T(8,128)(2,1)}, bf16[4,96,256]{2,1,0:T(8,128)(2,1)S(1)}, u32[]{:S(2)}, u32[]{:S(2)}) collective-permute-start(bf16[4,96,256]{2,1,0:T(8,128)(2,1)} %get-tuple-element.23), channel_id=1, source_target_pairs={{0,8},{1,9},{2,10},{3,11},{4,12},{5,13},{6,14},{7,15},{8,0},{9,1},... | collective-permute-start | bytes 589832 | tf_op jit(solution)/shard_map/ppermute | solution.py:290
  6.5 12.9 %collective-permute-start.2 = (bf16[4,96,256]{2,1,0:T(8,128)(2,1)}, bf16[4,96,256]{2,1,0:T(8,128)(2,1)S(1)}, u32[]{:S(2)}, u32[]{:S(2)}) collective-permute-start(bf16[4,96,256]{2,1,0:T(8,128)(2,1)} %get-tuple-element.24), channel_id=1, source_target_pairs={{0,12},{1,13},{2,14},{3,15},{4,8},{5,9},{6,10},{7,11},{8,4},{9,5},... | collective-permute-start | bytes 589832 | tf_op jit(solution)/shard_map/ppermute | solution.py:290
  10.2 9.2 %copy-start.1 = (bf16[4,96,256]{2,1,0:T(8,128)(2,1)S(1)}, bf16[4,96,256]{2,1,0:T(8,128)(2,1)}, u32[]{:S(2)}) copy-start(bf16[4,96,256]{2,1,0:T(8,128)(2,1)} %shard_map.41) | copy-start | bytes 589828
  12.2 38.8 %all-to-all-start = ((bf16[16,96,256]{2,1,0:T(8,128)(2,1)}), bf16[16,96,256]{2,1,0:T(8,128)(2,1)S(1)}, u32[]{:S(2)}, u32[]{:S(2)}) async-start(bf16[16,96,256]{2,1,0:T(8,128)(2,1)} %shard_map.39), calls=%async_computation | async-start | bytes 1572864 | tf_op jit(solution)/shard_map/all_to_all | solution.py:309
  19.6 16.9 %collective-permute-start.3 = (bf16[4,2,96,256]{3,2,0,1:T(8,128)(2,1)S(1)}, bf16[4,2,96,256]{3,2,0,1:T(8,128)(2,1)S(1)}, u32[]{:S(2)}, u32[]{:S(2)}) collective-permute-start(bf16[4,2,96,256]{3,2,0,1:T(8,128)(2,1)S(1)} %get-tuple-element.41), channel_id=1, source_target_pairs={{0,2},{1,3},{2,0},{3,1},{4,6},{5,7},{6,4},{7,5},{8,10},{9,11},{10,... | collective-permute-start | bytes 1179656 | tf_op jit(solution)/shard_map/ppermute | solution.py:290
  37.3 3.8 %collective-permute-start.4 = (bf16[8,96,256]{2,1,0:T(8,128)(2,1)}, bf16[8,96,256]{2,1,0:T(8,128)(2,1)S(1)}, u32[]{:S(2)}, u32[]{:S(2)}) collective-permute-start(bf16[8,96,256]{2,1,0:T(8,128)(2,1)} %bitcast.16), channel_id=1, source_target_pairs={{0,1},{1,0},{2,3},{3,2},{4,5},{5,4},{6,7},{7,6},{8,9},{9,8},{10,11... | collective-permute-start | bytes 1179656 | tf_op jit(solution)/shard_map/ppermute | solution.py:290
  43.4 9.9 %collective-permute-start.7 = (bf16[4,96,256]{2,1,0:T(8,128)(2,1)}, bf16[4,96,256]{2,1,0:T(8,128)(2,1)S(1)}, u32[]{:S(2)}, u32[]{:S(2)}) collective-permute-start(bf16[4,96,256]{2,1,0:T(8,128)(2,1)} %get-tuple-element.29), channel_id=1, source_target_pairs={{0,12},{1,13},{2,14},{3,15},{4,8},{5,9},{6,10},{7,11},{8,4},{9,5},... | collective-permute-start | bytes 589832 | tf_op jit(solution)/shard_map/ppermute | solution.py:290
  46.3 15.1 %collective-permute-start.5 = (bf16[4,96,256]{2,1,0:T(8,128)(2,1)}, bf16[4,96,256]{2,1,0:T(8,128)(2,1)S(1)}, u32[]{:S(2)}, u32[]{:S(2)}) collective-permute-start(bf16[4,96,256]{2,1,0:T(8,128)(2,1)} %get-tuple-element.27), channel_id=1, source_target_pairs={{0,4},{1,5},{2,6},{3,7},{4,0},{5,1},{6,2},{7,3},{8,12},{9,13},{10,... | collective-permute-start | bytes 589832 | tf_op jit(solution)/shard_map/ppermute | solution.py:290
  51.0 13.6 %collective-permute-start.6 = (bf16[4,96,256]{2,1,0:T(8,128)(2,1)}, bf16[4,96,256]{2,1,0:T(8,128)(2,1)S(1)}, u32[]{:S(2)}, u32[]{:S(2)}) collective-permute-start(bf16[4,96,256]{2,1,0:T(8,128)(2,1)} %get-tuple-element.28), channel_id=1, source_target_pairs={{0,8},{1,9},{2,10},{3,11},{4,12},{5,13},{6,14},{7,15},{8,0},{9,1},... | collective-permute-start | bytes 589832 | tf_op jit(solution)/shard_map/ppermute | solution.py:290
  53.3 29.1 %all-to-all-start.1 = ((bf16[16,96,256]{2,1,0:T(8,128)(2,1)}), bf16[16,96,256]{2,1,0:T(8,128)(2,1)S(1)}, u32[]{:S(2)}, u32[]{:S(2)}) async-start(bf16[16,96,256]{2,1,0:T(8,128)(2,1)} %shard_map.43), calls=%async_computation.1 | async-start | bytes 1572864 | tf_op jit(solution)/shard_map/all_to_all | solution.py:309
  64.7 17.0 %copy-start.2 = (bf16[15]{0:T(256)(128)(2,1)S(1)}, bf16[15]{0:T(256)(128)(2,1)}, u32[]{:S(2)}) copy-start(bf16[15]{0:T(256)(128)(2,1)} %param.5) | copy-start | bytes 94
  64.8 15.7 %collective-permute-start.8 = (bf16[4,2,96,256]{3,2,0,1:T(8,128)(2,1)S(1)}, bf16[4,2,96,256]{3,2,0,1:T(8,128)(2,1)S(1)}, u32[]{:S(2)}, u32[]{:S(2)}) collective-permute-start(bf16[4,2,96,256]{3,2,0,1:T(8,128)(2,1)S(1)} %get-tuple-element.37), channel_id=1, source_target_pairs={{0,2},{1,3},{2,0},{3,1},{4,6},{5,7},{6,4},{7,5},{8,10},{9,11},{10,... | collective-permute-start | bytes 1179656 | tf_op jit(solution)/shard_map/ppermute | solution.py:290
  80.6 3.2 %collective-permute-start.9 = (bf16[8,96,256]{2,1,0:T(8,128)(2,1)S(1)}, bf16[8,96,256]{2,1,0:T(8,128)(2,1)S(1)}, u32[]{:S(2)}, u32[]{:S(2)}) collective-permute-start(bf16[8,96,256]{2,1,0:T(8,128)(2,1)S(1)} %bitcast.53), channel_id=1, source_target_pairs={{0,1},{1,0},{2,3},{3,2},{4,5},{5,4},{6,7},{7,6},{8,9},{9,8},{10,11... | collective-permute-start | bytes 1179656 | tf_op jit(solution)/shard_map/ppermute | solution.py:290

commit v4 on v3

--- a/solution.py
+++ b/solution.py
@@ -323,7 +323,7 @@
     mine, _ = lax.optimization_barrier((mine, arrays[0]))
     arrays = far_hops(arrays, parts)
     done = zonal_first(circ, mine)
-    _, *after = lax.optimization_barrier((done, *arrays))
+    _, *after = lax.optimization_barrier(((done, band), *arrays))
     done, _ = lax.optimization_barrier((done, [arrays[3]]))
     back = swapped(done)
     blocks = near_hops(after, parts)

time: 85.6 us -> 85.1 us (level)
  transfers between devices with their start and end apart: 12 -> 12, of which waited for: 6 -> 7; matrix products, arithmetic and copies ran while one was open for 1% -> 1% of each run, Pallas kernels for 13% -> 13%
where the time goes in v4:
time: 85.1 us; the launch traced here: 84.4 us
  waiting for transfers between devices  36.9 us (43%)
  starting transfers between devices  32 us (38%)
  Pallas kernels  14.1 us (17%)
  other arithmetic  1.09 us (1%)
    ppermute x10, waiting for transfers between devices, hop(): return lax.ppermute(x, 'lon', [(i, i ^ distance) for i in range(parts)])  36.9 us
    ppermute x10, starting transfers between devices, hop(): return lax.ppermute(x, 'lon', [(i, i ^ distance) for i in range(parts)])  16.9 us
    all_to_all x2, starting transfers between devices, two_ways(): swapped = lambda x: lax.all_to_all(x, 'lon', 0, 0, tiled=True)  15.1 us
    pallas_call x2, Pallas kernels, second_half(): pl.pallas_call(functools.partial(second_half_kernel, first), in_specs=[SM...  3.6 us
    pallas_call x1, Pallas kernels, zonal_second(): pl.pallas_call(zonal_second_kernel, in_specs=[SMEM] + [VMEM] * 3, out_spe...  2.29 us
    pallas_call x1, Pallas kernels, zonal_first(): pl.pallas_call(zonal_first_kernel, in_specs=[VMEM, VMEM], out_specs=VMEM,...  2.28 us
    pallas_call x1, Pallas kernels, first_half(): pl.pallas_call(first_half_kernel, in_specs=[HBM], out_specs=VMEM, out_sha...  2.02 us
  transfers between devices with their start and end apart: 12, of which 7 were waited for; matrix products, arithmetic and copies ran while one was open for 1% of the time, Pallas kernels for 13%

profile of v4, /device:TPU:1, one launch (start us, length us, event | category | flops | bytes accessed | tf_op | source)
XLA Modules:
  0.0 84.4 jit_solution(9681751786820675797)
XLA Ops:
  0.0 2.0 %shard_map.40 = (bf16[4,96,256]{2,1,0:T(8,128)(2,1)}, bf16[4,96,256]{2,1,0:T(8,128)(2,1)}, bf16[4,96,256]{2,1,0:T(8,128)(2,1)}) custom-call(s32[1]{0:T(128)} %bitcast.me_ref, bf16[32,96,256]{2,1,0:T(8,128)(2,1)} %x_ref.4), custom_call_target="tpu_custom_call" | custom-call | tf_op jit(solution)/shard_map/pallas_call | solution.py:158
  2.0 2.2 %collective-permute-start = (bf16[4,96,256]{2,1,0:T(8,128)(2,1)}, bf16[4,96,256]{2,1,0:T(8,128)(2,1)S(1)}, u32[]{:S(2)}, u32[]{:S(2)}) collective-permute-start(bf16[4,96,256]{2,1,0:T(8,128)(2,1)} %get-tuple-element.20), channel_id=1, source_target_pairs={{0,4},{1,5},{2,6},{3,7},{4,0},{5,1},{6,2},{7,3},{8,12},{9,13},{10,... | collective-permute-start | bytes 589832 | tf_op jit(solution)/shard_map/ppermute | solution.py:290
  4.2 2.3 %collective-permute-start.1 = (bf16[4,96,256]{2,1,0:T(8,128)(2,1)}, bf16[4,96,256]{2,1,0:T(8,128)(2,1)S(1)}, u32[]{:S(2)}, u32[]{:S(2)}) collective-permute-start(bf16[4,96,256]{2,1,0:T(8,128)(2,1)} %get-tuple-element.23), channel_id=1, source_target_pairs={{0,8},{1,9},{2,10},{3,11},{4,12},{5,13},{6,14},{7,15},{8,0},{9,1},... | collective-permute-start | bytes 589832 | tf_op jit(solution)/shard_map/ppermute | solution.py:290
  6.5 2.0 %shard_map.39 = bf16[16,96,256]{2,1,0:T(8,128)(2,1)} custom-call(bf16[32,96,256]{2,1,0:T(8,128)(2,1)} %x_ref.4), custom_call_target="tpu_custom_call" | custom-call | tf_op jit(solution)/shard_map/pallas_call | solution.py:135
  8.6 1.6 %shard_map.41 = bf16[4,96,256]{2,1,0:T(8,128)(2,1)} custom-call(s32[1]{0:T(128)} %bitcast.me_ref, bf16[32,96,256]{2,1,0:T(8,128)(2,1)} %x_ref.4), custom_call_target="tpu_custom_call" | custom-call | tf_op jit(solution)/shard_map/pallas_call | solution.py:158
  10.2 2.0 %collective-permute-done = bf16[4,96,256]{2,1,0:T(8,128)(2,1)S(1)} collective-permute-done((bf16[4,96,256]{2,1,0:T(8,128)(2,1)}, bf16[4,96,256]{2,1,0:T(8,128)(2,1)S(1)}, u32[]{:S(2)}, u32[]{:S(2)}) %collective-permute-start) | collective-permute-done | bytes 196640 | tf_op jit(solution)/shard_map/ppermute | solution.py:290
  12.2 7.0 %all-to-all-start = ((bf16[16,96,256]{2,1,0:T(8,128)(2,1)}), bf16[16,96,256]{2,1,0:T(8,128)(2,1)S(1)}, u32[]{:S(2)}, u32[]{:S(2)}) async-start(bf16[16,96,256]{2,1,0:T(8,128)(2,1)} %shard_map.39), calls=%async_computation | async-start | bytes 1572864 | tf_op jit(solution)/shard_map/all_to_all | solution.py:309
  19.2 0.2 collective-permute-done.2
  19.4 0.1 pad_maximum_fusion
  19.5 0.1 slice_bitcast_fusion.2
  19.6 1.3 %collective-permute-start.3 = (bf16[4,2,96,256]{3,2,0,1:T(8,128)(2,1)S(1)}, bf16[4,2,96,256]{3,2,0,1:T(8,128)(2,1)S(1)}, u32[]{:S(2)}, u32[]{:S(2)}) collective-permute-start(bf16[4,2,96,256]{3,2,0,1:T(8,128)(2,1)S(1)} %get-tuple-element.41), channel_id=1, source_target_pairs={{0,2},{1,3},{2,0},{3,1},{4,6},{5,7},{6,4},{7,5},{8,10},{9,11},{10,... | collective-permute-start | bytes 1179656 | tf_op jit(solution)/shard_map/ppermute | solution.py:290
  20.9 15.6 %collective-permute-done.3 = bf16[4,2,96,256]{3,2,0,1:T(8,128)(2,1)S(1)} collective-permute-done((bf16[4,2,96,256]{3,2,0,1:T(8,128)(2,1)S(1)}, bf16[4,2,96,256]{3,2,0,1:T(8,128)(2,1)S(1)}, u32[]{:S(2)}, u32[]{:S(2)}) %collective-permute-start.3) | collective-permute-done | bytes 393248 | tf_op jit(solution)/shard_map/ppermute | solution.py:290
  36.5 0.8 pad_maximum_fusion.3
  37.3 2.2 %collective-permute-start.4 = (bf16[8,96,256]{2,1,0:T(8,128)(2,1)}, bf16[8,96,256]{2,1,0:T(8,128)(2,1)S(1)}, u32[]{:S(2)}, u32[]{:S(2)}) collective-permute-start(bf16[8,96,256]{2,1,0:T(8,128)(2,1)} %bitcast.16), channel_id=1, source_target_pairs={{0,1},{1,0},{2,3},{3,2},{4,5},{5,4},{6,7},{7,6},{8,9},{9,8},{10,11... | collective-permute-start | bytes 1179656 | tf_op jit(solution)/shard_map/ppermute | solution.py:290
  39.6 0.5 shard_map.38.circ_ref
  40.1 1.0 %collective-permute-done.4.refs_1_ = bf16[8,96,256]{2,1,0:T(8,128)(2,1)S(1)} collective-permute-done((bf16[8,96,256]{2,1,0:T(8,128)(2,1)}, bf16[8,96,256]{2,1,0:T(8,128)(2,1)S(1)}, u32[]{:S(2)}, u32[]{:S(2)}) %collective-permute-start.4) | collective-permute-done | bytes 393248 | tf_op jit(solution)/shard_map/ppermute | solution.py:290
  41.1 2.3 %shard_map.42 = (bf16[4,96,256]{2,1,0:T(8,128)(2,1)S(1)}, bf16[4,96,256]{2,1,0:T(8,128)(2,1)}, bf16[4,96,256]{2,1,0:T(8,128)(2,1)}, bf16[4,96,256]{2,1,0:T(8,128)(2,1)}) custom-call(s32[1]{0:T(128)} %bitcast.me_ref, bf16[2,1536,256]{2,1,0:T(8,128)(2,1)S(1)} %shard_map.38.circ_ref, bf16[8,96,256]{2,1,0:T(8,128)(2,1)S(1)} %bitcast.49, ...), custom_call_target="tpu_custom_call" | custom-call | flops 4831838208 | bytes 4718592 | tf_op jit(solution)/shard_map/pallas_call | solution.py:223
  43.4 2.9 %collective-permute-start.7 = (bf16[4,96,256]{2,1,0:T(8,128)(2,1)}, bf16[4,96,256]{2,1,0:T(8,128)(2,1)S(1)}, u32[]{:S(2)}, u32[]{:S(2)}) collective-permute-start(bf16[4,96,256]{2,1,0:T(8,128)(2,1)} %get-tuple-element.29), channel_id=1, source_target_pairs={{0,12},{1,13},{2,14},{3,15},{4,8},{5,9},{6,10},{7,11},{8,4},{9,5},... | collective-permute-start | bytes 589832 | tf_op jit(solution)/shard_map/ppermute | solution.py:290
  46.3 4.7 %collective-permute-start.5 = (bf16[4,96,256]{2,1,0:T(8,128)(2,1)}, bf16[4,96,256]{2,1,0:T(8,128)(2,1)S(1)}, u32[]{:S(2)}, u32[]{:S(2)}) collective-permute-start(bf16[4,96,256]{2,1,0:T(8,128)(2,1)} %get-tuple-element.27), channel_id=1, source_target_pairs={{0,4},{1,5},{2,6},{3,7},{4,0},{5,1},{6,2},{7,3},{8,12},{9,13},{10,... | collective-permute-start | bytes 589832 | tf_op jit(solution)/shard_map/ppermute | solution.py:290
  51.0 2.3 %shard_map.43 = bf16[16,96,256]{2,1,0:T(8,128)(2,1)} custom-call(bf16[2,1536,256]{2,1,0:T(8,128)(2,1)S(1)} %shard_map.38.circ_ref, bf16[16,96,256]{2,1,0:T(8,128)(2,1)S(1)} %all-to-all-done.x_ref), custom_call_target="tpu_custom_call" | custom-call | flops 1207959552 | bytes 4718592 | tf_op jit(solution)/shard_map/pallas_call | solution.py:189
  53.3 8.1 %all-to-all-start.1 = ((bf16[16,96,256]{2,1,0:T(8,128)(2,1)}), bf16[16,96,256]{2,1,0:T(8,128)(2,1)S(1)}, u32[]{:S(2)}, u32[]{:S(2)}) async-start(bf16[16,96,256]{2,1,0:T(8,128)(2,1)} %shard_map.43), calls=%async_computation.1 | async-start | bytes 1572864 | tf_op jit(solution)/shard_map/all_to_all | solution.py:309
  61.5 0.8 shard_map.37.band_ref
  62.3 2.3 %collective-permute-done.6 = bf16[4,96,256]{2,1,0:T(8,128)(2,1)S(1)} collective-permute-done((bf16[4,96,256]{2,1,0:T(8,128)(2,1)}, bf16[4,96,256]{2,1,0:T(8,128)(2,1)S(1)}, u32[]{:S(2)}, u32[]{:S(2)}) %collective-permute-start.6) | collective-permute-done | bytes 196640 | tf_op jit(solution)/shard_map/ppermute | solution.py:290
  64.6 0.1 pad_maximum_fusion.1
  64.7 0.1 slice_bitcast_fusion
  64.8 0.1 collective-permute-start.8
  64.9 15.6 %collective-permute-done.8 = bf16[4,2,96,256]{3,2,0,1:T(8,128)(2,1)S(1)} collective-permute-done((bf16[4,2,96,256]{3,2,0,1:T(8,128)(2,1)S(1)}, bf16[4,2,96,256]{3,2,0,1:T(8,128)(2,1)S(1)}, u32[]{:S(2)}, u32[]{:S(2)}) %collective-permute-start.8) | collective-permute-done | bytes 393248 | tf_op jit(solution)/shard_map/ppermute | solution.py:290
  80.5 0.1 pad_maximum_fusion.2
  80.6 1.1 %collective-permute-start.9 = (bf16[8,96,256]{2,1,0:T(8,128)(2,1)S(1)}, bf16[8,96,256]{2,1,0:T(8,128)(2,1)S(1)}, u32[]{:S(2)}, u32[]{:S(2)}) collective-permute-start(bf16[8,96,256]{2,1,0:T(8,128)(2,1)S(1)} %bitcast.53), channel_id=1, source_target_pairs={{0,1},{1,0},{2,3},{3,2},{4,5},{5,4},{6,7},{7,6},{8,9},{9,8},{10,11... | collective-permute-start | bytes 1179656 | tf_op jit(solution)/shard_map/ppermute | solution.py:290
  81.7 1.3 %shard_map.44.refs_2_ = bf16[32,96,256]{2,1,0:T(8,128)(2,1)} custom-call(bf16[256,256]{1,0:T(8,128)(2,1)S(1)} %shard_map.37.band_ref, bf16[16,96,256]{2,1,0:T(8,128)(2,1)S(1)} %all-to-all-done.1.x_ref), custom_call_target="tpu_custom_call" | custom-call | tf_op jit(solution)/shard_map/pallas_call | solution.py:243
  83.0 0.1 collective-permute-done.9.refs_1_
  83.0 1.4 %shard_map.45 = bf16[32,96,256]{2,1,0:T(8,128)(2,1)} custom-call(s32[1]{0:T(128)} %bitcast.me_ref, bf16[256,256]{1,0:T(8,128)(2,1)S(1)} %shard_map.37.band_ref, bf16[8,96,256]{2,1,0:T(8,128)(2,1)S(1)} %bitcast.48, bf16[8,96,256]{2,1,0:T(8,128)(2,1)S(1)} %collective-permute-done.9.refs_1_, ...), custom_call_target="tpu_custom_call", output_to_operand_aliasing={{}: (4, {})} | custom-call | tf_op jit(solution)/shard_map/pallas_call | solution.py:275
  (16 shorter events, 0.1 us)
Async XLA Ops:
  0.0 39.6 %copy-start = (bf16[32,1536]{1,0:T(8,128)(2,1)S(1)}, bf16[32,1536]{1,0:T(8,128)(2,1)}, u32[]{:S(2)}) copy-start(bf16[32,1536]{1,0:T(8,128)(2,1)} %param.4) | copy-start | bytes 294916
  2.0 10.2 %collective-permute-start = (bf16[4,96,256]{2,1,0:T(8,128)(2,1)}, bf16[4,96,256]{2,1,0:T(8,128)(2,1)S(1)}, u32[]{:S(2)}, u32[]{:S(2)}) collective-permute-start(bf16[4,96,256]{2,1,0:T(8,128)(2,1)} %get-tuple-element.20), channel_id=1, source_target_pairs={{0,4},{1,5},{2,6},{3,7},{4,0},{5,1},{6,2},{7,3},{8,12},{9,13},{10,... | collective-permute-start | bytes 589832 | tf_op jit(solution)/shard_map/ppermute | solution.py:290
  4.2 15.0 %collective-permute-start.1 = (bf16[4,96,256]{2,1,0:T(8,128)(2,1)}, bf16[4,96,256]{2,1,0:T(8,128)(2,1)S(1)}, u32[]{:S(2)}, u32[]{:S(2)}) collective-permute-start(bf16[4,96,256]{2,1,0:T(8,128)(2,1)} %get-tuple-element.23), channel_id=1, source_target_pairs={{0,8},{1,9},{2,10},{3,11},{4,12},{5,13},{6,14},{7,15},{8,0},{9,1},... | collective-permute-start | bytes 589832 | tf_op jit(solution)/shard_map/ppermute | solution.py:290
  6.5 12.9 %collective-permute-start.2 = (bf16[4,96,256]{2,1,0:T(8,128)(2,1)}, bf16[4,96,256]{2,1,0:T(8,128)(2,1)S(1)}, u32[]{:S(2)}, u32[]{:S(2)}) collective-permute-start(bf16[4,96,256]{2,1,0:T(8,128)(2,1)} %get-tuple-element.24), channel_id=1, source_target_pairs={{0,12},{1,13},{2,14},{3,15},{4,8},{5,9},{6,10},{7,11},{8,4},{9,5},... | collective-permute-start | bytes 589832 | tf_op jit(solution)/shard_map/ppermute | solution.py:290
  10.2 9.2 %copy-start.1 = (bf16[4,96,256]{2,1,0:T(8,128)(2,1)S(1)}, bf16[4,96,256]{2,1,0:T(8,128)(2,1)}, u32[]{:S(2)}) copy-start(bf16[4,96,256]{2,1,0:T(8,128)(2,1)} %shard_map.41) | copy-start | bytes 589828
  12.2 38.8 %all-to-all-start = ((bf16[16,96,256]{2,1,0:T(8,128)(2,1)}), bf16[16,96,256]{2,1,0:T(8,128)(2,1)S(1)}, u32[]{:S(2)}, u32[]{:S(2)}) async-start(bf16[16,96,256]{2,1,0:T(8,128)(2,1)} %shard_map.39), calls=%async_computation | async-start | bytes 1572864 | tf_op jit(solution)/shard_map/all_to_all | solution.py:309
  19.6 16.9 %collective-permute-start.3 = (bf16[4,2,96,256]{3,2,0,1:T(8,128)(2,1)S(1)}, bf16[4,2,96,256]{3,2,0,1:T(8,128)(2,1)S(1)}, u32[]{:S(2)}, u32[]{:S(2)}) collective-permute-start(bf16[4,2,96,256]{3,2,0,1:T(8,128)(2,1)S(1)} %get-tuple-element.41), channel_id=1, source_target_pairs={{0,2},{1,3},{2,0},{3,1},{4,6},{5,7},{6,4},{7,5},{8,10},{9,11},{10,... | collective-permute-start | bytes 1179656 | tf_op jit(solution)/shard_map/ppermute | solution.py:290
  37.3 3.8 %collective-permute-start.4 = (bf16[8,96,256]{2,1,0:T(8,128)(2,1)}, bf16[8,96,256]{2,1,0:T(8,128)(2,1)S(1)}, u32[]{:S(2)}, u32[]{:S(2)}) collective-permute-start(bf16[8,96,256]{2,1,0:T(8,128)(2,1)} %bitcast.16), channel_id=1, source_target_pairs={{0,1},{1,0},{2,3},{3,2},{4,5},{5,4},{6,7},{7,6},{8,9},{9,8},{10,11... | collective-permute-start | bytes 1179656 | tf_op jit(solution)/shard_map/ppermute | solution.py:290
  43.4 9.9 %collective-permute-start.7 = (bf16[4,96,256]{2,1,0:T(8,128)(2,1)}, bf16[4,96,256]{2,1,0:T(8,128)(2,1)S(1)}, u32[]{:S(2)}, u32[]{:S(2)}) collective-permute-start(bf16[4,96,256]{2,1,0:T(8,128)(2,1)} %get-tuple-element.29), channel_id=1, source_target_pairs={{0,12},{1,13},{2,14},{3,15},{4,8},{5,9},{6,10},{7,11},{8,4},{9,5},... | collective-permute-start | bytes 589832 | tf_op jit(solution)/shard_map/ppermute | solution.py:290
  46.3 15.9 %collective-permute-start.5 = (bf16[4,96,256]{2,1,0:T(8,128)(2,1)}, bf16[4,96,256]{2,1,0:T(8,128)(2,1)S(1)}, u32[]{:S(2)}, u32[]{:S(2)}) collective-permute-start(bf16[4,96,256]{2,1,0:T(8,128)(2,1)} %get-tuple-element.27), channel_id=1, source_target_pairs={{0,4},{1,5},{2,6},{3,7},{4,0},{5,1},{6,2},{7,3},{8,12},{9,13},{10,... | collective-permute-start | bytes 589832 | tf_op jit(solution)/shard_map/ppermute | solution.py:290
  51.0 13.6 %collective-permute-start.6 = (bf16[4,96,256]{2,1,0:T(8,128)(2,1)}, bf16[4,96,256]{2,1,0:T(8,128)(2,1)S(1)}, u32[]{:S(2)}, u32[]{:S(2)}) collective-permute-start(bf16[4,96,256]{2,1,0:T(8,128)(2,1)} %get-tuple-element.28), channel_id=1, source_target_pairs={{0,8},{1,9},{2,10},{3,11},{4,12},{5,13},{6,14},{7,15},{8,0},{9,1},... | collective-permute-start | bytes 589832 | tf_op jit(solution)/shard_map/ppermute | solution.py:290
  53.3 8.1 %copy-start.2 = (bf16[15]{0:T(256)(128)(2,1)S(1)}, bf16[15]{0:T(256)(128)(2,1)}, u32[]{:S(2)}) copy-start(bf16[15]{0:T(256)(128)(2,1)} %param.5) | copy-start | bytes 94
  53.3 28.4 %all-to-all-start.1 = ((bf16[16,96,256]{2,1,0:T(8,128)(2,1)}), bf16[16,96,256]{2,1,0:T(8,128)(2,1)S(1)}, u32[]{:S(2)}, u32[]{:S(2)}) async-start(bf16[16,96,256]{2,1,0:T(8,128)(2,1)} %shard_map.43), calls=%async_computation.1 | async-start | bytes 1572864 | tf_op jit(solution)/shard_map/all_to_all | solution.py:309
  64.8 15.7 %collective-permute-start.8 = (bf16[4,2,96,256]{3,2,0,1:T(8,128)(2,1)S(1)}, bf16[4,2,96,256]{3,2,0,1:T(8,128)(2,1)S(1)}, u32[]{:S(2)}, u32[]{:S(2)}) collective-permute-start(bf16[4,2,96,256]{3,2,0,1:T(8,128)(2,1)S(1)} %get-tuple-element.37), channel_id=1, source_target_pairs={{0,2},{1,3},{2,0},{3,1},{4,6},{5,7},{6,4},{7,5},{8,10},{9,11},{10,... | collective-permute-start | bytes 1179656 | tf_op jit(solution)/shard_map/ppermute | solution.py:290
  80.6 2.5 %collective-permute-start.9 = (bf16[8,96,256]{2,1,0:T(8,128)(2,1)S(1)}, bf16[8,96,256]{2,1,0:T(8,128)(2,1)S(1)}, u32[]{:S(2)}, u32[]{:S(2)}) collective-permute-start(bf16[8,96,256]{2,1,0:T(8,128)(2,1)S(1)} %bitcast.53), channel_id=1, source_target_pairs={{0,1},{1,0},{2,3},{3,2},{4,5},{5,4},{6,7},{7,6},{8,9},{9,8},{10,11... | collective-permute-start | bytes 1179656 | tf_op jit(solution)/shard_map/ppermute | solution.py:290

commit v5 on v4

--- a/solution.py
+++ b/solution.py
@@ -11,7 +11,7 @@
 TAPS = 15
 LANES = 128
 WIDE = 256
-STEPS = 2
+STEPS = 1
 NEAR = 4
 HBM = pl.BlockSpec(memory_space=pltpu.HBM)
 VMEM = pl.BlockSpec(memory_space=pltpu.VMEM)

time: 85.1 us -> 85.1 us (level)
  no operation moved by 1% of the time
where the time goes in v5:
time: 85.1 us; the launch traced here: 84.4 us
  waiting for transfers between devices  37 us (43%)
  starting transfers between devices  32 us (38%)
  Pallas kernels  14.1 us (17%)
  other arithmetic  1.09 us (1%)
    ppermute x10, waiting for transfers between devices, hop(): return lax.ppermute(x, 'lon', [(i, i ^ distance) for i in range(parts)])  37 us
    ppermute x10, starting transfers between devices, hop(): return lax.ppermute(x, 'lon', [(i, i ^ distance) for i in range(parts)])  16.9 us
    all_to_all x2, starting transfers between devices, two_ways(): swapped = lambda x: lax.all_to_all(x, 'lon', 0, 0, tiled=True)  15.1 us
    pallas_call x2, Pallas kernels, second_half(): pl.pallas_call(functools.partial(second_half_kernel, first), in_specs=[SM...  3.6 us
    pallas_call x1, Pallas kernels, zonal_second(): pl.pallas_call(zonal_second_kernel, in_specs=[SMEM] + [VMEM] * 3, out_spe...  2.29 us
    pallas_call x1, Pallas kernels, zonal_first(): pl.pallas_call(zonal_first_kernel, in_specs=[VMEM, VMEM], out_specs=VMEM,...  2.28 us
    pallas_call x1, Pallas kernels, first_half(): pl.pallas_call(first_half_kernel, in_specs=[HBM], out_specs=VMEM, out_sha...  2.02 us
  transfers between devices with their start and end apart: 12, of which 7 were waited for; matrix products, arithmetic and copies ran while one was open for 1% of the time, Pallas kernels for 13%

profile of v5, /device:TPU:1, one launch (start us, length us, event | category | flops | bytes accessed | tf_op | source)
XLA Modules:
  0.0 84.4 jit_solution(6160708640991119681)
XLA Ops:
  0.0 2.0 %shard_map.40 = (bf16[4,96,256]{2,1,0:T(8,128)(2,1)}, bf16[4,96,256]{2,1,0:T(8,128)(2,1)}, bf16[4,96,256]{2,1,0:T(8,128)(2,1)}) custom-call(s32[1]{0:T(128)} %bitcast.me_ref, bf16[32,96,256]{2,1,0:T(8,128)(2,1)} %x_ref.4), custom_call_target="tpu_custom_call" | custom-call | tf_op jit(solution)/shard_map/pallas_call | solution.py:158
  2.0 2.2 %collective-permute-start = (bf16[4,96,256]{2,1,0:T(8,128)(2,1)}, bf16[4,96,256]{2,1,0:T(8,128)(2,1)S(1)}, u32[]{:S(2)}, u32[]{:S(2)}) collective-permute-start(bf16[4,96,256]{2,1,0:T(8,128)(2,1)} %get-tuple-element.20), channel_id=1, source_target_pairs={{0,4},{1,5},{2,6},{3,7},{4,0},{5,1},{6,2},{7,3},{8,12},{9,13},{10,... | collective-permute-start | bytes 589832 | tf_op jit(solution)/shard_map/ppermute | solution.py:290
  4.2 2.3 %collective-permute-start.1 = (bf16[4,96,256]{2,1,0:T(8,128)(2,1)}, bf16[4,96,256]{2,1,0:T(8,128)(2,1)S(1)}, u32[]{:S(2)}, u32[]{:S(2)}) collective-permute-start(bf16[4,96,256]{2,1,0:T(8,128)(2,1)} %get-tuple-element.23), channel_id=1, source_target_pairs={{0,8},{1,9},{2,10},{3,11},{4,12},{5,13},{6,14},{7,15},{8,0},{9,1},... | collective-permute-start | bytes 589832 | tf_op jit(solution)/shard_map/ppermute | solution.py:290
  6.5 2.0 %shard_map.39 = bf16[16,96,256]{2,1,0:T(8,128)(2,1)} custom-call(bf16[32,96,256]{2,1,0:T(8,128)(2,1)} %x_ref.4), custom_call_target="tpu_custom_call" | custom-call | tf_op jit(solution)/shard_map/pallas_call | solution.py:135
  8.6 1.6 %shard_map.41 = bf16[4,96,256]{2,1,0:T(8,128)(2,1)} custom-call(s32[1]{0:T(128)} %bitcast.me_ref, bf16[32,96,256]{2,1,0:T(8,128)(2,1)} %x_ref.4), custom_call_target="tpu_custom_call" | custom-call | tf_op jit(solution)/shard_map/pallas_call | solution.py:158
  10.2 2.0 %collective-permute-done = bf16[4,96,256]{2,1,0:T(8,128)(2,1)S(1)} collective-permute-done((bf16[4,96,256]{2,1,0:T(8,128)(2,1)}, bf16[4,96,256]{2,1,0:T(8,128)(2,1)S(1)}, u32[]{:S(2)}, u32[]{:S(2)}) %collective-permute-start) | collective-permute-done | bytes 196640 | tf_op jit(solution)/shard_map/ppermute | solution.py:290
  12.2 7.0 %all-to-all-start = ((bf16[16,96,256]{2,1,0:T(8,128)(2,1)}), bf16[16,96,256]{2,1,0:T(8,128)(2,1)S(1)}, u32[]{:S(2)}, u32[]{:S(2)}) async-start(bf16[16,96,256]{2,1,0:T(8,128)(2,1)} %shard_map.39), calls=%async_computation | async-start | bytes 1572864 | tf_op jit(solution)/shard_map/all_to_all | solution.py:309
  19.2 0.2 collective-permute-done.2
  19.4 0.1 pad_maximum_fusion
  19.5 0.1 slice_bitcast_fusion.2
  19.6 1.3 %collective-permute-start.3 = (bf16[4,2,96,256]{3,2,0,1:T(8,128)(2,1)S(1)}, bf16[4,2,96,256]{3,2,0,1:T(8,128)(2,1)S(1)}, u32[]{:S(2)}, u32[]{:S(2)}) collective-permute-start(bf16[4,2,96,256]{3,2,0,1:T(8,128)(2,1)S(1)} %get-tuple-element.41), channel_id=1, source_target_pairs={{0,2},{1,3},{2,0},{3,1},{4,6},{5,7},{6,4},{7,5},{8,10},{9,11},{10,... | collective-permute-start | bytes 1179656 | tf_op jit(solution)/shard_map/ppermute | solution.py:290
  20.9 15.6 %collective-permute-done.3 = bf16[4,2,96,256]{3,2,0,1:T(8,128)(2,1)S(1)} collective-permute-done((bf16[4,2,96,256]{3,2,0,1:T(8,128)(2,1)S(1)}, bf16[4,2,96,256]{3,2,0,1:T(8,128)(2,1)S(1)}, u32[]{:S(2)}, u32[]{:S(2)}) %collective-permute-start.3) | collective-permute-done | bytes 393248 | tf_op jit(solution)/shard_map/ppermute | solution.py:290
  36.5 0.8 pad_maximum_fusion.3
  37.3 2.2 %collective-permute-start.4 = (bf16[8,96,256]{2,1,0:T(8,128)(2,1)}, bf16[8,96,256]{2,1,0:T(8,128)(2,1)S(1)}, u32[]{:S(2)}, u32[]{:S(2)}) collective-permute-start(bf16[8,96,256]{2,1,0:T(8,128)(2,1)} %bitcast.16), channel_id=1, source_target_pairs={{0,1},{1,0},{2,3},{3,2},{4,5},{5,4},{6,7},{7,6},{8,9},{9,8},{10,11... | collective-permute-start | bytes 1179656 | tf_op jit(solution)/shard_map/ppermute | solution.py:290
  39.6 0.5 shard_map.38.circ_ref
  40.1 1.0 %collective-permute-done.4.refs_1_ = bf16[8,96,256]{2,1,0:T(8,128)(2,1)S(1)} collective-permute-done((bf16[8,96,256]{2,1,0:T(8,128)(2,1)}, bf16[8,96,256]{2,1,0:T(8,128)(2,1)S(1)}, u32[]{:S(2)}, u32[]{:S(2)}) %collective-permute-start.4) | collective-permute-done | bytes 393248 | tf_op jit(solution)/shard_map/ppermute | solution.py:290
  41.1 2.3 %shard_map.42 = (bf16[4,96,256]{2,1,0:T(8,128)(2,1)S(1)}, bf16[4,96,256]{2,1,0:T(8,128)(2,1)}, bf16[4,96,256]{2,1,0:T(8,128)(2,1)}, bf16[4,96,256]{2,1,0:T(8,128)(2,1)}) custom-call(s32[1]{0:T(128)} %bitcast.me_ref, bf16[2,1536,256]{2,1,0:T(8,128)(2,1)S(1)} %shard_map.38.circ_ref, bf16[8,96,256]{2,1,0:T(8,128)(2,1)S(1)} %bitcast.49, ...), custom_call_target="tpu_custom_call" | custom-call | flops 4831838208 | bytes 4718592 | tf_op jit(solution)/shard_map/pallas_call | solution.py:223
  43.4 2.9 %collective-permute-start.7 = (bf16[4,96,256]{2,1,0:T(8,128)(2,1)}, bf16[4,96,256]{2,1,0:T(8,128)(2,1)S(1)}, u32[]{:S(2)}, u32[]{:S(2)}) collective-permute-start(bf16[4,96,256]{2,1,0:T(8,128)(2,1)} %get-tuple-element.29), channel_id=1, source_target_pairs={{0,12},{1,13},{2,14},{3,15},{4,8},{5,9},{6,10},{7,11},{8,4},{9,5},... | collective-permute-start | bytes 589832 | tf_op jit(solution)/shard_map/ppermute | solution.py:290
  46.3 4.7 %collective-permute-start.5 = (bf16[4,96,256]{2,1,0:T(8,128)(2,1)}, bf16[4,96,256]{2,1,0:T(8,128)(2,1)S(1)}, u32[]{:S(2)}, u32[]{:S(2)}) collective-permute-start(bf16[4,96,256]{2,1,0:T(8,128)(2,1)} %get-tuple-element.27), channel_id=1, source_target_pairs={{0,4},{1,5},{2,6},{3,7},{4,0},{5,1},{6,2},{7,3},{8,12},{9,13},{10,... | collective-permute-start | bytes 589832 | tf_op jit(solution)/shard_map/ppermute | solution.py:290
  51.0 2.3 %shard_map.43 = bf16[16,96,256]{2,1,0:T(8,128)(2,1)} custom-call(bf16[2,1536,256]{2,1,0:T(8,128)(2,1)S(1)} %shard_map.38.circ_ref, bf16[16,96,256]{2,1,0:T(8,128)(2,1)S(1)} %all-to-all-done.x_ref), custom_call_target="tpu_custom_call" | custom-call | flops 1207959552 | bytes 4718592 | tf_op jit(solution)/shard_map/pallas_call | solution.py:189
  53.3 8.1 %all-to-all-start.1 = ((bf16[16,96,256]{2,1,0:T(8,128)(2,1)}), bf16[16,96,256]{2,1,0:T(8,128)(2,1)S(1)}, u32[]{:S(2)}, u32[]{:S(2)}) async-start(bf16[16,96,256]{2,1,0:T(8,128)(2,1)} %shard_map.43), calls=%async_computation.1 | async-start | bytes 1572864 | tf_op jit(solution)/shard_map/all_to_all | solution.py:309
  61.5 0.8 shard_map.37.band_ref
  62.3 2.3 %collective-permute-done.6 = bf16[4,96,256]{2,1,0:T(8,128)(2,1)S(1)} collective-permute-done((bf16[4,96,256]{2,1,0:T(8,128)(2,1)}, bf16[4,96,256]{2,1,0:T(8,128)(2,1)S(1)}, u32[]{:S(2)}, u32[]{:S(2)}) %collective-permute-start.6) | collective-permute-done | bytes 196640 | tf_op jit(solution)/shard_map/ppermute | solution.py:290
  64.6 0.1 pad_maximum_fusion.1
  64.7 0.1 slice_bitcast_fusion
  64.8 0.1 collective-permute-start.8
  64.9 15.6 %collective-permute-done.8 = bf16[4,2,96,256]{3,2,0,1:T(8,128)(2,1)S(1)} collective-permute-done((bf16[4,2,96,256]{3,2,0,1:T(8,128)(2,1)S(1)}, bf16[4,2,96,256]{3,2,0,1:T(8,128)(2,1)S(1)}, u32[]{:S(2)}, u32[]{:S(2)}) %collective-permute-start.8) | collective-permute-done | bytes 393248 | tf_op jit(solution)/shard_map/ppermute | solution.py:290
  80.5 0.1 pad_maximum_fusion.2
  80.6 1.1 %collective-permute-start.9 = (bf16[8,96,256]{2,1,0:T(8,128)(2,1)S(1)}, bf16[8,96,256]{2,1,0:T(8,128)(2,1)S(1)}, u32[]{:S(2)}, u32[]{:S(2)}) collective-permute-start(bf16[8,96,256]{2,1,0:T(8,128)(2,1)S(1)} %bitcast.53), channel_id=1, source_target_pairs={{0,1},{1,0},{2,3},{3,2},{4,5},{5,4},{6,7},{7,6},{8,9},{9,8},{10,11... | collective-permute-start | bytes 1179656 | tf_op jit(solution)/shard_map/ppermute | solution.py:290
  81.7 1.3 %shard_map.44.refs_2_ = bf16[32,96,256]{2,1,0:T(8,128)(2,1)} custom-call(bf16[256,256]{1,0:T(8,128)(2,1)S(1)} %shard_map.37.band_ref, bf16[16,96,256]{2,1,0:T(8,128)(2,1)S(1)} %all-to-all-done.1.x_ref), custom_call_target="tpu_custom_call" | custom-call | tf_op jit(solution)/shard_map/pallas_call | solution.py:243
  82.9 0.1 collective-permute-done.9.refs_1_
  83.0 1.4 %shard_map.45 = bf16[32,96,256]{2,1,0:T(8,128)(2,1)} custom-call(s32[1]{0:T(128)} %bitcast.me_ref, bf16[256,256]{1,0:T(8,128)(2,1)S(1)} %shard_map.37.band_ref, bf16[8,96,256]{2,1,0:T(8,128)(2,1)S(1)} %bitcast.48, bf16[8,96,256]{2,1,0:T(8,128)(2,1)S(1)} %collective-permute-done.9.refs_1_, ...), custom_call_target="tpu_custom_call", output_to_operand_aliasing={{}: (4, {})} | custom-call | tf_op jit(solution)/shard_map/pallas_call | solution.py:275
  (16 shorter events, 0.1 us)
Async XLA Ops:
  0.0 39.6 %copy-start = (bf16[32,1536]{1,0:T(8,128)(2,1)S(1)}, bf16[32,1536]{1,0:T(8,128)(2,1)}, u32[]{:S(2)}) copy-start(bf16[32,1536]{1,0:T(8,128)(2,1)} %param.4) | copy-start | bytes 294916
  2.0 10.2 %collective-permute-start = (bf16[4,96,256]{2,1,0:T(8,128)(2,1)}, bf16[4,96,256]{2,1,0:T(8,128)(2,1)S(1)}, u32[]{:S(2)}, u32[]{:S(2)}) collective-permute-start(bf16[4,96,256]{2,1,0:T(8,128)(2,1)} %get-tuple-element.20), channel_id=1, source_target_pairs={{0,4},{1,5},{2,6},{3,7},{4,0},{5,1},{6,2},{7,3},{8,12},{9,13},{10,... | collective-permute-start | bytes 589832 | tf_op jit(solution)/shard_map/ppermute | solution.py:290
  4.2 15.0 %collective-permute-start.1 = (bf16[4,96,256]{2,1,0:T(8,128)(2,1)}, bf16[4,96,256]{2,1,0:T(8,128)(2,1)S(1)}, u32[]{:S(2)}, u32[]{:S(2)}) collective-permute-start(bf16[4,96,256]{2,1,0:T(8,128)(2,1)} %get-tuple-element.23), channel_id=1, source_target_pairs={{0,8},{1,9},{2,10},{3,11},{4,12},{5,13},{6,14},{7,15},{8,0},{9,1},... | collective-permute-start | bytes 589832 | tf_op jit(solution)/shard_map/ppermute | solution.py:290
  6.5 12.9 %collective-permute-start.2 = (bf16[4,96,256]{2,1,0:T(8,128)(2,1)}, bf16[4,96,256]{2,1,0:T(8,128)(2,1)S(1)}, u32[]{:S(2)}, u32[]{:S(2)}) collective-permute-start(bf16[4,96,256]{2,1,0:T(8,128)(2,1)} %get-tuple-element.24), channel_id=1, source_target_pairs={{0,12},{1,13},{2,14},{3,15},{4,8},{5,9},{6,10},{7,11},{8,4},{9,5},... | collective-permute-start | bytes 589832 | tf_op jit(solution)/shard_map/ppermute | solution.py:290
  10.2 9.2 %copy-start.1 = (bf16[4,96,256]{2,1,0:T(8,128)(2,1)S(1)}, bf16[4,96,256]{2,1,0:T(8,128)(2,1)}, u32[]{:S(2)}) copy-start(bf16[4,96,256]{2,1,0:T(8,128)(2,1)} %shard_map.41) | copy-start | bytes 589828
  12.2 38.8 %all-to-all-start = ((bf16[16,96,256]{2,1,0:T(8,128)(2,1)}), bf16[16,96,256]{2,1,0:T(8,128)(2,1)S(1)}, u32[]{:S(2)}, u32[]{:S(2)}) async-start(bf16[16,96,256]{2,1,0:T(8,128)(2,1)} %shard_map.39), calls=%async_computation | async-start | bytes 1572864 | tf_op jit(solution)/shard_map/all_to_all | solution.py:309
  19.6 16.9 %collective-permute-start.3 = (bf16[4,2,96,256]{3,2,0,1:T(8,128)(2,1)S(1)}, bf16[4,2,96,256]{3,2,0,1:T(8,128)(2,1)S(1)}, u32[]{:S(2)}, u32[]{:S(2)}) collective-permute-start(bf16[4,2,96,256]{3,2,0,1:T(8,128)(2,1)S(1)} %get-tuple-element.41), channel_id=1, source_target_pairs={{0,2},{1,3},{2,0},{3,1},{4,6},{5,7},{6,4},{7,5},{8,10},{9,11},{10,... | collective-permute-start | bytes 1179656 | tf_op jit(solution)/shard_map/ppermute | solution.py:290
  37.3 3.8 %collective-permute-start.4 = (bf16[8,96,256]{2,1,0:T(8,128)(2,1)}, bf16[8,96,256]{2,1,0:T(8,128)(2,1)S(1)}, u32[]{:S(2)}, u32[]{:S(2)}) collective-permute-start(bf16[8,96,256]{2,1,0:T(8,128)(2,1)} %bitcast.16), channel_id=1, source_target_pairs={{0,1},{1,0},{2,3},{3,2},{4,5},{5,4},{6,7},{7,6},{8,9},{9,8},{10,11... | collective-permute-start | bytes 1179656 | tf_op jit(solution)/shard_map/ppermute | solution.py:290
  43.4 9.9 %collective-permute-start.7 = (bf16[4,96,256]{2,1,0:T(8,128)(2,1)}, bf16[4,96,256]{2,1,0:T(8,128)(2,1)S(1)}, u32[]{:S(2)}, u32[]{:S(2)}) collective-permute-start(bf16[4,96,256]{2,1,0:T(8,128)(2,1)} %get-tuple-element.29), channel_id=1, source_target_pairs={{0,12},{1,13},{2,14},{3,15},{4,8},{5,9},{6,10},{7,11},{8,4},{9,5},... | collective-permute-start | bytes 589832 | tf_op jit(solution)/shard_map/ppermute | solution.py:290
  46.3 15.9 %collective-permute-start.5 = (bf16[4,96,256]{2,1,0:T(8,128)(2,1)}, bf16[4,96,256]{2,1,0:T(8,128)(2,1)S(1)}, u32[]{:S(2)}, u32[]{:S(2)}) collective-permute-start(bf16[4,96,256]{2,1,0:T(8,128)(2,1)} %get-tuple-element.27), channel_id=1, source_target_pairs={{0,4},{1,5},{2,6},{3,7},{4,0},{5,1},{6,2},{7,3},{8,12},{9,13},{10,... | collective-permute-start | bytes 589832 | tf_op jit(solution)/shard_map/ppermute | solution.py:290
  51.0 13.6 %collective-permute-start.6 = (bf16[4,96,256]{2,1,0:T(8,128)(2,1)}, bf16[4,96,256]{2,1,0:T(8,128)(2,1)S(1)}, u32[]{:S(2)}, u32[]{:S(2)}) collective-permute-start(bf16[4,96,256]{2,1,0:T(8,128)(2,1)} %get-tuple-element.28), channel_id=1, source_target_pairs={{0,8},{1,9},{2,10},{3,11},{4,12},{5,13},{6,14},{7,15},{8,0},{9,1},... | collective-permute-start | bytes 589832 | tf_op jit(solution)/shard_map/ppermute | solution.py:290
  53.3 8.1 %copy-start.2 = (bf16[15]{0:T(256)(128)(2,1)S(1)}, bf16[15]{0:T(256)(128)(2,1)}, u32[]{:S(2)}) copy-start(bf16[15]{0:T(256)(128)(2,1)} %param.5) | copy-start | bytes 94
  53.3 28.4 %all-to-all-start.1 = ((bf16[16,96,256]{2,1,0:T(8,128)(2,1)}), bf16[16,96,256]{2,1,0:T(8,128)(2,1)S(1)}, u32[]{:S(2)}, u32[]{:S(2)}) async-start(bf16[16,96,256]{2,1,0:T(8,128)(2,1)} %shard_map.43), calls=%async_computation.1 | async-start | bytes 1572864 | tf_op jit(solution)/shard_map/all_to_all | solution.py:309
  64.8 15.7 %collective-permute-start.8 = (bf16[4,2,96,256]{3,2,0,1:T(8,128)(2,1)S(1)}, bf16[4,2,96,256]{3,2,0,1:T(8,128)(2,1)S(1)}, u32[]{:S(2)}, u32[]{:S(2)}) collective-permute-start(bf16[4,2,96,256]{3,2,0,1:T(8,128)(2,1)S(1)} %get-tuple-element.37), channel_id=1, source_target_pairs={{0,2},{1,3},{2,0},{3,1},{4,6},{5,7},{6,4},{7,5},{8,10},{9,11},{10,... | collective-permute-start | bytes 1179656 | tf_op jit(solution)/shard_map/ppermute | solution.py:290
  80.6 2.5 %collective-permute-start.9 = (bf16[8,96,256]{2,1,0:T(8,128)(2,1)S(1)}, bf16[8,96,256]{2,1,0:T(8,128)(2,1)S(1)}, u32[]{:S(2)}, u32[]{:S(2)}) collective-permute-start(bf16[8,96,256]{2,1,0:T(8,128)(2,1)S(1)} %bitcast.53), channel_id=1, source_target_pairs={{0,1},{1,0},{2,3},{3,2},{4,5},{5,4},{6,7},{7,6},{8,9},{9,8},{10,11... | collective-permute-start | bytes 1179656 | tf_op jit(solution)/shard_map/ppermute | solution.py:290
